TPU v7x, 32 devices: a whole 2x2x4 slice. The times are simulated.
32 devices in a mesh: graph: 8 (over z, y), feat: 4 (over x, core).
Axes of the slice: x: 2, y: 2, z: 4, core: 2. Of those that a mesh axis runs over, the one named last changes fastest.
Arguments:
- features: bfloat16 [16384, 1024], P('graph', 'feat'), may hold values from -6 to 6
- w_self: bfloat16 [1024, 1024], replicated, may hold values from -0.1875 to 0.1875
- w_neigh: bfloat16 [1024, 1024], replicated, may hold values from -0.1875 to 0.1875
- adjacency: bfloat16 [256, 128, 128], P('graph'), may hold values from 0 to 1.5, as said below
- block_source: int32 [256], P('graph'), may hold values from 0 to 15
- block_to_slot: int32 [256], P('graph'), may hold values from 0 to 15
- send_rows: int32 [8, 8, 256], P('graph'), may hold values from 0 to 2047
- send_counts: int32 [8, 8], P('graph'), may hold values from 64 to 256, as said below
- degree: int32 [16384], P('graph'), may hold values from 8 to 32
- cotangent: bfloat16 [16384, 1024], P('graph', 'feat'), may hold values from -6 to 6
Outputs:
- hidden_out: bfloat16 [16384, 1024], P('graph', 'feat')
- grad_features: bfloat16 [16384, 1024], P('graph', 'feat')
- grad_self: float32 [1024, 1024], P('feat')
- grad_neigh: float32 [1024, 1024], P('feat')
Inputs may be any that keep to these rules, and one draw needn't show every extreme that they name: Slots 0 to send_counts[p, q] - 1 from p to q are live; in every draw some partition receives 256 live slots from every partition. `adjacency`: edge weights; a block is mostly zeros.
All inputs are finite; a program needn't handle non-finite values.
Results may differ from a plain program's by a relative error of at most 0.0066.
Values may be sent and summed in bfloat16 or wider, within the bound.
A program may use at most 128 MiB of HBM per device.

v0:
```python
import jax
import jax.numpy as jnp
from jax import lax
from jax.sharding import PartitionSpec as P


def silu_slope(values):
    sig = jax.nn.sigmoid(values)
    return sig * (1.0 + values * (1.0 - sig))


def on_device(
    features,
    w_self,
    w_neigh,
    adjacency,
    block_source,
    block_to_slot,
    send_rows,
    send_counts,
    degree,
    cotangent,
):
    node_rows, feat_cols = features.shape
    part_count = lax.axis_size("graph")
    block_size = adjacency.shape[1]
    slot_cap = send_rows.shape[2]
    slot_total = part_count * slot_cap // block_size
    source_count = node_rows // block_size
    column_start = lax.axis_index("feat") * feat_cols
    sources = features.reshape(source_count, block_size, feat_cols)
    picked = jnp.take(sources, block_source, axis=0)
    prods = jnp.einsum("kij,kjd->kid", adjacency, picked, preferred_element_type=jnp.float32)
    slot_sums = jax.ops.segment_sum(prods, block_to_slot, num_segments=slot_total)
    live_counts = send_counts[0]
    is_live = jnp.arange(slot_cap, dtype=jnp.int32)[None, :] < live_counts[:, None]
    outgoing = jnp.where(
        is_live[:, :, None], slot_sums.reshape(part_count, slot_cap, feat_cols), 0.0
    ).astype(jnp.bfloat16)
    row_ids = jnp.where(is_live, send_rows[0], -1)
    incoming, incoming_ids = (
        lax.all_to_all(outgoing, "graph", split_axis=0, concat_axis=0, tiled=True),
        lax.all_to_all(row_ids, "graph", split_axis=0, concat_axis=0, tiled=True),
    )
    valid_slot = incoming_ids >= 0
    target_rows = jnp.where(valid_slot, incoming_ids, node_rows).reshape(-1)
    neighbor_sum = (
        jnp.zeros((node_rows, feat_cols), jnp.float32)
        .at[target_rows]
        .add(incoming.reshape(-1, feat_cols).astype(jnp.float32), mode="drop")
    )
    degrees = degree.astype(jnp.float32)[:, None]
    neighbor_mean = (neighbor_sum / degrees).astype(jnp.bfloat16)
    self_rows = lax.dynamic_slice_in_dim(w_self, column_start, feat_cols, 0)
    neigh_rows = lax.dynamic_slice_in_dim(w_neigh, column_start, feat_cols, 0)
    own_term = lax.dot_general(
        self_rows, features, (((0,), (1,)), ((), ())), preferred_element_type=jnp.float32
    )
    agg_term = lax.dot_general(
        neigh_rows, neighbor_mean, (((0,), (1,)), ((), ())), preferred_element_type=jnp.float32
    )
    pre_act = lax.psum_scatter(own_term + agg_term, "feat", scatter_dimension=0, tiled=True).T
    hidden_out = jax.nn.silu(pre_act).astype(jnp.bfloat16)
    grad_pre = (cotangent.astype(jnp.float32) * silu_slope(pre_act)).astype(jnp.bfloat16)
    grad_full = lax.all_gather(grad_pre, "feat", axis=1, tiled=True)
    local_self = lax.dot_general(
        features, grad_full, (((0,), (0,)), ((), ())), preferred_element_type=jnp.float32
    )
    local_neigh = lax.dot_general(
        neighbor_mean, grad_full, (((0,), (0,)), ((), ())), preferred_element_type=jnp.float32
    )
    grad_self, grad_neigh = lax.psum((local_self, local_neigh), "graph")
    self_grad = lax.dot_general(
        grad_full, self_rows, (((1,), (1,)), ((), ())), preferred_element_type=jnp.float32
    )
    back_rows = (
        lax.dot_general(
            grad_full, neigh_rows, (((1,), (1,)), ((), ())), preferred_element_type=jnp.float32
        )
        / degrees
    ).astype(jnp.bfloat16)
    lookup = jnp.where(valid_slot, incoming_ids, 0)
    sending_back = jnp.where(valid_slot[:, :, None], jnp.take(back_rows, lookup, axis=0), 0.0)
    returned = lax.all_to_all(sending_back, "graph", split_axis=0, concat_axis=0, tiled=True)
    slot_blocks = returned.reshape(slot_total, block_size, feat_cols)
    chosen = jnp.take(slot_blocks, block_to_slot, axis=0)
    contrib = jnp.einsum("kij,kid->kjd", adjacency, chosen, preferred_element_type=jnp.float32)
    neigh_grad = jax.ops.segment_sum(contrib, block_source, num_segments=source_count).reshape(
        node_rows, feat_cols
    )
    grad_features = (self_grad + neigh_grad).astype(jnp.bfloat16)
    return (hidden_out, grad_features, grad_self, grad_neigh)


def solution(mesh):
    placed = (
        P("graph", "feat"),
        P(),
        P(),
        P("graph", None, None),
        P("graph"),
        P("graph"),
        P("graph", None, None),
        P("graph", None),
        P("graph"),
        P("graph", "feat"),
    )
    return jax.shard_map(
        on_device,
        mesh=mesh,
        in_specs=placed,
        out_specs=(P("graph", "feat"), P("graph", "feat"), P("feat", None), P("feat", None)),
        check_vma=False,
    )
```

profile of v0, /device:TPU:0, one launch (start us, length us, event | category | flops | bytes accessed | tf_op | source)
XLA Modules:
  0.0 355.0 jit_solution(4032134557099491881)
XLA Ops:
  7.2 0.0 copy-start
  7.2 1.5 compare_select_fusion.4
  8.7 7.3 %all-to-all-start = ((s32[8,1,256]{2,1,0:T(1,128)}), s32[8,1,256]{2,1,0:T(1,128)S(1)}, u32[]{:S(2)}, u32[]{:S(2)}) async-start(s32[8,1,256]{2,1,0:T(1,128)} %compare_select_fusion.4), calls=%async_computation | async-start | bytes 16384 | tf_op jit(solution)/shard_map/all_to_all | solution.py:43
  16.0 0.7 iota_compare_fusion
  16.7 0.7 compare_select_fusion.7
  17.4 0.7 compare_and_fusion.2
  18.0 0.0 copy-start.6
  18.1 3.3 gather_fusion.1
  21.4 4.4 %convolution_bitcast_fusion.1 = f32[32,128,256]{1,2,0:T(8,128)} fusion(bf16[32,128,128]{2,1,0:T(8,128)(2,1)S(1)} %copy-done.6, bf16[32,128,256]{2,1,0:T(8,128)(2,1)} %gather_fusion.1, pred[32]{0:T(512)(128)(4,1)S(1)} %compare_and_fusion.2), kind=kOutput, calls=%fused_computation.12 | convolution fusion | flops 269484032 | bytes 7340064 | tf_op jit(solution)/shard_map/kij,kjd->kid/dot_general | solution.py:33
  25.8 5.6 %copy.27 = f32[32,128,256]{2,1,0:T(8,128)} copy(f32[32,128,256]{1,2,0:T(8,128)} %convolution_bitcast_fusion.1) | data formatting | bytes 8388608 | tf_op jit(solution)/shard_map/kij,kjd->kid/dot_general | solution.py:33
  31.4 1.6 broadcast.122.clone
  33.0 9.7 %scatter_fusion = f32[16,128,256]{2,1,0:T(8,128)} fusion(f32[16,128,256]{2,1,0:T(8,128)} %broadcast.122.clone, s32[32]{0:T(128)S(1)} %copy-done.10, f32[32,128,256]{2,1,0:T(8,128)} %copy.27), kind=kCustom, calls=%fused_computation.3 | custom fusion | flops 1048576 | bytes 12583040 | tf_op jit(solution)/shard_map/scatter-add | solution.py:34
  42.7 2.6 fusion.12
  45.3 6.0 %all-to-all-start.1 = ((bf16[8,256,256]{2,1,0:T(8,128)(2,1)}), bf16[8,256,256]{2,1,0:T(8,128)(2,1)}, u32[]{:S(2)}, u32[]{:S(2)}) async-start(bf16[8,256,256]{2,1,0:T(8,128)(2,1)} %fusion.12), calls=%async_computation.1 | async-start | bytes 2097152 | tf_op jit(solution)/shard_map/all_to_all | solution.py:42
  51.3 0.0 reduce-scatter.2.cloned.1.call-start
  51.4 5.6 %fusion.23 = f32[1024,2048]{1,0:T(8,128)} fusion(bf16[2048,256]{1,0:T(8,128)(2,1)S(1)} %copy-done.2, bf16[1024,1024]{1,0:T(8,128)(2,1)} %param.13, s32[]{:T(128)S(6)} %select_n.85), kind=kOutput, calls=%fused_computation.41 | convolution fusion | flops 1073741824 | bytes 9961476 | tf_op jit(solution)/shard_map/dot_general | solution.py:56
  57.0 19.8 %all-to-all-done.1 = bf16[8,256,256]{2,1,0:T(8,128)(2,1)} async-done(((bf16[8,256,256]{2,1,0:T(8,128)(2,1)}), bf16[8,256,256]{2,1,0:T(8,128)(2,1)}, u32[]{:S(2)}, u32[]{:S(2)}) %all-to-all-start.1) | async-done | bytes 1048608 | tf_op jit(solution)/shard_map/all_to_all | solution.py:42
  76.9 12.4 %scatter_custom_fusion.1 = f32[2048,256]{1,0:T(8,128)} fusion(s32[2048]{0:T(1024)S(1)} %bitcast.71, bf16[2048,256]{1,0:T(8,128)(2,1)} %bitcast.15, f32[]{:T(128)} %constant.16.clone.1), kind=kCustom, calls=%fused_computation.13 | custom fusion | flops 1048576 | bytes 3145732 | tf_op jit(solution)/shard_map/scatter-add | solution.py:50
  89.3 8.9 %convolution_add_fusion = f32[1024,2048]{1,0:T(8,128)} fusion(f32[1024,2048]{1,0:T(8,128)} %fusion.23, bf16[1024,1024]{1,0:T(8,128)(2,1)S(1)} %copy-done, s32[]{:T(128)S(6)} %select_n.85, f32[2048,256]{1,0:T(8,128)} %scatter_custom_fusion.1, f32[2048]{0:T(1024)S(1)} %convert_element_type.35), kind=kOutput, calls=%fused_computation.6 | convolution fusion | flops 1076887552 | bytes 19406852 | tf_op jit(solution)/shard_map/dot_general | solution.py:59
  98.2 0.0 reduce-scatter.2.cloned.1.call-update
  98.2 0.2 all-gather.2.cloned.1.call-start
  98.4 1.5 copy.28
  99.9 68.9 %reduce-scatter.2.cloned.1.call-done = f32[256,2048]{1,0:T(8,128)} async-done(((f32[1024,2048]{1,0:T(8,128)}), f32[256,2048]{1,0:T(8,128)}) %reduce-scatter.2.cloned.1.call-update) | async-done | bytes 2097168 | tf_op jit(solution)/shard_map/reduce_scatter | solution.py:62
  168.9 3.9 %fusion.11 = (bf16[2048,256]{0,1:T(8,128)(2,1)}, bf16[2048,256]{0,1:T(8,128)(2,1)}) fusion(f32[256,2048]{1,0:T(8,128)} %reduce-scatter.2.cloned.1.call-done, bf16[2048,256]{0,1:T(8,128)(2,1)S(1)} %copy.28), kind=kLoop, calls=%fused_computation.25 | loop fusion | flops 6291456 | bytes 5242880 | tf_op jit(solution)/shard_map/convert_element_type | solution.py:64
  172.7 0.0 all-gather.2.cloned.1.call-update
  172.8 34.6 %all-gather.2.cloned.1.call-done = bf16[2048,1024]{0,1:T(8,128)(2,1)} async-done(((bf16[2048,256]{0,1:T(8,128)(2,1)}), bf16[2048,1024]{0,1:T(8,128)(2,1)}) %all-gather.2.cloned.1.call-update) | async-done | bytes 4194320 | tf_op jit(solution)/shard_map/all_gather | solution.py:65
  207.4 3.6 %fusion.1 = bf16[2048,256]{1,0:T(8,128)(2,1)S(1)} fusion(bf16[2048,1024]{0,1:T(8,128)(2,1)} %all-gather.2.cloned.1.call-done, f32[2048]{0:T(1024)S(1)} %convert_element_type.35, bf16[1024,1024]{1,0:T(8,128)(2,1)S(1)} %copy-done, s32[]{:T(128)S(6)} %select_n.85), kind=kOutput, calls=%fused_computation.10 | convolution fusion | flops 1074790400 | bytes 5775364 | tf_op jit(solution)/shard_map/dot_general | solution.py:77
  211.0 7.5 %gather_fusion = bf16[2048,256]{1,0:T(8,128)(2,1)S(1)} fusion(bf16[2048,256]{1,0:T(8,128)(2,1)S(1)} %fusion.1, s32[2048]{0:T(1024)S(1)} %broadcast_clamp_fusion), kind=kCustom, calls=%fused_computation.2 | custom fusion | bytes 2105344 | tf_op jit(solution)/shard_map/jit(_take)/gather | solution.py:83
  218.5 0.0 copy-start.3
  218.5 1.5 select_select_fusion
  220.1 5.5 %all-to-all-start.2 = ((bf16[8,256,256]{2,1,0:T(8,128)(2,1)}), bf16[8,256,256]{2,1,0:T(8,128)(2,1)S(1)}, u32[]{:S(2)}, u32[]{:S(2)}) async-start(bf16[8,256,256]{2,1,0:T(8,128)(2,1)} %select_select_fusion), calls=%async_computation.3 | async-start | bytes 2097152 | tf_op jit(solution)/shard_map/all_to_all | solution.py:84
  225.6 0.0 all-reduce.3.cloned.1.call-start
  225.6 4.6 %convolution_bitcast_fusion.2 = f32[256,1024]{0,1:T(8,128)} fusion(bf16[2048,1024]{0,1:T(8,128)(2,1)} %all-gather.2.cloned.1.call-done, bf16[2048,256]{1,0:T(8,128)(2,1)S(1)} %copy-done.3), kind=kOutput, calls=%fused_computation.33 | convolution fusion | flops 1073741824 | bytes 6291456 | tf_op jit(solution)/shard_map/dot_general | solution.py:66
  230.3 2.7 fusion.31
  233.0 0.0 all-reduce.3.cloned.1.call-update
  233.0 1.2 copy-done.5
  234.2 1.3 copy.31
  235.5 30.0 %all-to-all-done.2 = bf16[8,256,256]{2,1,0:T(8,128)(2,1)S(1)} async-done(((bf16[8,256,256]{2,1,0:T(8,128)(2,1)}), bf16[8,256,256]{2,1,0:T(8,128)(2,1)S(1)}, u32[]{:S(2)}, u32[]{:S(2)}) %all-to-all-start.2) | async-done | bytes 1048608 | tf_op jit(solution)/shard_map/all_to_all | solution.py:84
  265.4 2.1 gather_fusion.2
  267.5 4.4 %convolution_bitcast_fusion = f32[32,128,256]{1,2,0:T(8,128)} fusion(bf16[32,128,128]{2,1,0:T(8,128)(2,1)S(1)} %copy-done.7, bf16[32,128,256]{2,1,0:T(8,128)(2,1)} %gather_fusion.2, pred[32]{0:T(512)(128)(4,1)S(1)} %compare_and_fusion.1), kind=kOutput, calls=%fused_computation.11 | convolution fusion | flops 269484032 | bytes 7340064 | tf_op jit(solution)/shard_map/kij,kid->kjd/dot_general | solution.py:87
  271.9 5.6 %copy.30 = f32[32,128,256]{2,1,0:T(8,128)} copy(f32[32,128,256]{1,2,0:T(8,128)} %convolution_bitcast_fusion) | data formatting | bytes 8388608 | tf_op jit(solution)/shard_map/kij,kid->kjd/dot_general | solution.py:87
  277.6 0.2 broadcast.122
  277.8 0.5 copy-done.11
  278.2 6.5 %scatter_fusion.1 = f32[16,128,256]{2,1,0:T(8,128)S(1)} fusion(f32[16,128,256]{2,1,0:T(8,128)S(1)} %broadcast.122, s32[32]{0:T(128)S(1)} %copy-done.11, f32[32,128,256]{2,1,0:T(8,128)} %copy.30), kind=kCustom, calls=%fused_computation.5 | custom fusion | flops 1048576 | bytes 12583040 | tf_op jit(solution)/shard_map/scatter-add | solution.py:88
  284.8 4.7 %fusion = bf16[2048,256]{1,0:T(8,128)(2,1)} fusion(f32[2048,256]{1,0:T(8,128)S(1)} %bitcast.65, bf16[2048,1024]{0,1:T(8,128)(2,1)} %all-gather.2.cloned.1.call-done, bf16[1024,1024]{1,0:T(8,128)(2,1)} %param.13, s32[]{:T(128)S(6)} %select_n.85), kind=kOutput, calls=%fused_computation.8 | convolution fusion | flops 1074790400 | bytes 7864324 | tf_op jit(solution)/shard_map/dot_general | solution.py:73
  289.5 55.3 %all-reduce.3.cloned.1.call-done = (f32[256,1024]{0,1:T(8,128)}, f32[256,1024]{1,0:T(8,128)}) async-done(((f32[256,1024]{0,1:T(8,128)}, f32[256,1024]{1,0:T(8,128)}), (f32[256,1024]{0,1:T(8,128)}, f32[256,1024]{1,0:T(8,128)})) %all-reduce.3.cloned.1.call-update) | async-done | bytes 2097168 | tf_op jit(solution)/shard_map/psum | solution.py:72
  344.8 2.7 copy.32
  347.5 1.0 copy.45
  (31 shorter events, 0.1 us)
Async XLA Ops:
  7.2 82.1 %copy-start = (bf16[1024,1024]{1,0:T(8,128)(2,1)S(1)}, bf16[1024,1024]{1,0:T(8,128)(2,1)}, u32[]{:S(2)}) copy-start(bf16[1024,1024]{1,0:T(8,128)(2,1)} %param.14) | copy-start | bytes 6291460
  8.7 36.6 %all-to-all-start = ((s32[8,1,256]{2,1,0:T(1,128)}), s32[8,1,256]{2,1,0:T(1,128)S(1)}, u32[]{:S(2)}, u32[]{:S(2)}) async-start(s32[8,1,256]{2,1,0:T(1,128)} %compare_select_fusion.4), calls=%async_computation | async-start | bytes 16384 | tf_op jit(solution)/shard_map/all_to_all | solution.py:43
  18.0 3.4 copy-start.6
  31.4 1.6 copy-start.10
  42.7 8.7 %copy-start.9 = (s32[2048]{0:T(1024)S(1)}, s32[2048]{0:T(1024)}, u32[]{:S(2)}) copy-start(s32[2048]{0:T(1024)} %param.20) | copy-start | bytes 24580
  42.7 8.7 %copy-start.2 = (bf16[2048,256]{1,0:T(8,128)(2,1)S(1)}, bf16[2048,256]{1,0:T(8,128)(2,1)}, u32[]{:S(2)}) copy-start(bf16[2048,256]{1,0:T(8,128)(2,1)} %param.12) | copy-start | bytes 3145732
  45.3 31.6 %all-to-all-start.1 = ((bf16[8,256,256]{2,1,0:T(8,128)(2,1)}), bf16[8,256,256]{2,1,0:T(8,128)(2,1)}, u32[]{:S(2)}, u32[]{:S(2)}) async-start(bf16[8,256,256]{2,1,0:T(8,128)(2,1)} %fusion.12), calls=%async_computation.1 | async-start | bytes 2097152 | tf_op jit(solution)/shard_map/all_to_all | solution.py:42
  51.3 117.5 %reduce-scatter.2.cloned.1.call-start = ((), (), s32[]{:S(2)}) async-start(), calls=%async_computation.4 | async-start | bytes 10485760 | tf_op jit(solution)/shard_map/reduce_scatter | solution.py:62
  98.2 109.2 %all-gather.2.cloned.1.call-start = ((), (), s32[]{:S(2)}) async-start(), calls=%async_computation.5 | async-start | bytes 5242880 | tf_op jit(solution)/shard_map/all_gather | solution.py:65
  218.5 7.1 %copy-start.3 = (bf16[2048,256]{1,0:T(8,128)(2,1)S(1)}, bf16[2048,256]{1,0:T(8,128)(2,1)}, u32[]{:S(2)}) copy-start(bf16[2048,256]{1,0:T(8,128)(2,1)} %param.12) | copy-start | bytes 3145732
  220.1 45.4 %all-to-all-start.2 = ((bf16[8,256,256]{2,1,0:T(8,128)(2,1)}), bf16[8,256,256]{2,1,0:T(8,128)(2,1)S(1)}, u32[]{:S(2)}, u32[]{:S(2)}) async-start(bf16[8,256,256]{2,1,0:T(8,128)(2,1)} %select_select_fusion), calls=%async_computation.3 | async-start | bytes 2097152 | tf_op jit(solution)/shard_map/all_to_all | solution.py:84
  225.6 119.2 %all-reduce.3.cloned.1.call-start = ((), (), s32[]{:S(2)}) async-start(), calls=%async_computation.6 | async-start | bytes 4194304 | tf_op jit(solution)/shard_map/psum | solution.py:72
  225.6 4.7 %copy-start.4 = (f32[2048,256]{1,0:T(8,128)S(1)}, f32[2048,256]{1,0:T(8,128)}, u32[]{:S(2)}) copy-start(f32[2048,256]{1,0:T(8,128)} %scatter_custom_fusion.1) | copy-start | bytes 6291460
  225.6 4.6 %copy-start.12 = (bf16[2048,1024]{0,1:T(8,128)(2,1)S(1)}, bf16[2048,1024]{0,1:T(8,128)(2,1)}, u32[]{:S(2)}) copy-start(bf16[2048,1024]{0,1:T(8,128)(2,1)} %all-gather.2.cloned.1.call-done) | copy-start | bytes 12582916
  233.0 1.2 copy-start.5
  265.4 2.1 copy-start.7
  277.6 0.7 copy-start.11
  344.8 2.7 copy-start.8
  344.8 3.7 %copy-start.1 = (bf16[1024,1024]{1,0:T(8,128)(2,1)S(1)}, bf16[1024,1024]{1,0:T(8,128)(2,1)}, u32[]{:S(2)}) copy-start(bf16[1024,1024]{1,0:T(8,128)(2,1)} %param.14) | copy-start | bytes 6291460
Sparse Core Ops, SparseCore 0:
  98.3 70.5 reduce-scatter.1
  172.9 34.4 all-gather.1
  233.1 111.6 all-reduce.2
where the time goes:
time: 356 us; the launch traced here: 355 us
  waiting for transfers between devices  209 us (59%)
  other arithmetic  40.2 us (11%)
  matrix products  39 us (11%)
  local copies, waits for them, and re-layouts  34 us (10%)
  starting transfers between devices  19.1 us (5%)
  between operations  13.9 us (4%)
    reduce_scatter x1, waiting for transfers between devices, on_device(): lax.psum_scatter(own_term + agg_term, 'feat', scatter_dimension=0, tiled=...  68.9 us
    psum x1, waiting for transfers between devices, on_device(): grad_self, grad_neigh = lax.psum((local_self, local_neigh), 'graph')  55.3 us
    all_gather x1, waiting for transfers between devices, on_device(): grad_full = lax.all_gather(grad_pre, 'feat', axis=1, tiled=True)  34.6 us
    all_to_all x1, waiting for transfers between devices, on_device(): lax.all_to_all(sending_back, 'graph', split_axis=0, concat_axis=0, tiled=...  30 us
    all_to_all x1, waiting for transfers between devices, on_device(): lax.all_to_all(outgoing, 'graph', split_axis=0, concat_axis=0, tiled=True)  19.8 us
    scatter-add x1, other arithmetic, on_device(): neighbor_sum = jnp.zeros((node_rows, feat_cols), jnp.float32).at[target_r...  12.4 us
    scatter-add x1, other arithmetic, on_device(): jax.ops.segment_sum(prods, block_to_slot, num_segments=slot_total)  9.67 us
    dot_general x1, matrix products, on_device(): lax.dot_general(neigh_rows, neighbor_mean, (((0,), (1,)), ((), ())), pref...  8.9 us
  transfers between devices with their start and end apart: 6, of which 5 were waited for; matrix products, arithmetic and copies ran while one was open for 19% of the time, Pallas kernels for 0%

commit v1 on v0

v1 whole, which is shorter than its diff:
```python
import functools

import jax
import jax.numpy as jnp
from jax import lax
from jax.experimental import pallas as pl
from jax.experimental.pallas import tpu as pltpu
from jax.sharding import PartitionSpec as P

SMEM = pltpu.SMEM
VMEM = pltpu.VMEM
GROUP = 4


def silu_slope(values):
    sig = jax.nn.sigmoid(values)
    return sig * (1.0 + values * (1.0 - sig))


def collect_kernel(source_ref, slot_ref, count_ref, adj_ref, feat_ref, out_ref, acc):
    blocks, block, _ = adj_ref.shape
    slot_total = out_ref.shape[0]
    halves = slot_total // count_ref.shape[1]
    acc[...] = jnp.zeros_like(acc)

    def add(step, carry):
        prods = []
        for j in range(GROUP):
            k = step * GROUP + j
            rows = pl.ds(pl.multiple_of(source_ref[k] * block, block), block)
            prods.append(jnp.dot(adj_ref[k], feat_ref[rows, :], preferred_element_type=jnp.float32))
        for j in range(GROUP):
            acc[slot_ref[step * GROUP + j]] += prods[j]
        return carry

    lax.fori_loop(0, blocks // GROUP, add, 0)

    def finish(s, carry):
        limit = count_ref[0, s // halves] - (s % halves) * block
        rows = lax.broadcasted_iota(jnp.int32, out_ref.shape[1:], 0)
        out_ref[s] = jnp.where(rows < limit, acc[s], 0.0).astype(jnp.bfloat16)
        return carry

    lax.fori_loop(0, slot_total, finish, 0)


def collect(block_source, block_to_slot, send_counts, adjacency, features, slot_total):
    blocks, block, _ = adjacency.shape
    shape = (slot_total, block, features.shape[1])
    return pl.pallas_call(
        collect_kernel,
        out_shape=jax.ShapeDtypeStruct(shape, jnp.bfloat16),
        in_specs=[pl.BlockSpec(memory_space=SMEM)] * 3 + [pl.BlockSpec(memory_space=VMEM)] * 2,
        out_specs=pl.BlockSpec(memory_space=VMEM),
        scratch_shapes=[pltpu.VMEM(shape, jnp.float32)],
        compiler_params=pltpu.CompilerParams(vmem_limit_bytes=32 * 2**20),
        name="collect",
    )(block_source, block_to_slot, send_counts, adjacency, features)


def spread_kernel(source_ref, slot_ref, adj_ref, ret_ref, grad_ref, w_ref, out_ref, acc):
    blocks, block, _ = adj_ref.shape
    sources = out_ref.shape[0] // block

    def start(b, carry):
        rows = pl.ds(pl.multiple_of(b * block, block), block)
        acc[b] = lax.dot_general(
            grad_ref[rows, :], w_ref[...], (((1,), (1,)), ((), ())),
            preferred_element_type=jnp.float32,
        )
        return carry

    lax.fori_loop(0, sources, start, 0)

    def add(step, carry):
        prods = []
        for j in range(GROUP):
            k = step * GROUP + j
            prods.append(lax.dot_general(
                adj_ref[k], ret_ref[slot_ref[k]], (((0,), (0,)), ((), ())),
                preferred_element_type=jnp.float32,
            ))
        for j in range(GROUP):
            acc[source_ref[step * GROUP + j]] += prods[j]
        return carry

    lax.fori_loop(0, blocks // GROUP, add, 0)

    def finish(b, carry):
        rows = pl.ds(pl.multiple_of(b * block, block), block)
        out_ref[rows, :] = acc[b].astype(jnp.bfloat16)
        return carry

    lax.fori_loop(0, sources, finish, 0)


def spread(block_source, block_to_slot, adjacency, returned, grad_full, self_rows):
    blocks, block, _ = adjacency.shape
    nodes = grad_full.shape[0]
    cols = returned.shape[2]
    return pl.pallas_call(
        spread_kernel,
        out_shape=jax.ShapeDtypeStruct((nodes, cols), jnp.bfloat16),
        in_specs=[pl.BlockSpec(memory_space=SMEM)] * 2 + [pl.BlockSpec(memory_space=VMEM)] * 4,
        out_specs=pl.BlockSpec(memory_space=VMEM),
        scratch_shapes=[pltpu.VMEM((nodes // block, block, cols), jnp.float32)],
        compiler_params=pltpu.CompilerParams(vmem_limit_bytes=40 * 2**20),
        name="spread",
    )(block_source, block_to_slot, adjacency, returned, grad_full, self_rows)


def on_device(
    features,
    w_self,
    w_neigh,
    adjacency,
    block_source,
    block_to_slot,
    send_rows,
    send_counts,
    degree,
    cotangent,
):
    node_rows, feat_cols = features.shape
    part_count = lax.axis_size("graph")
    block_size = adjacency.shape[1]
    slot_cap = send_rows.shape[2]
    slot_total = part_count * slot_cap // block_size
    column_start = lax.axis_index("feat") * feat_cols
    feat_full = lax.all_gather(features, "feat", axis=1, tiled=True)
    outgoing = collect(block_source, block_to_slot, send_counts, adjacency, features, slot_total)
    is_live = jnp.arange(slot_cap, dtype=jnp.int32)[None, :] < send_counts[0][:, None]
    row_ids = jnp.where(is_live, send_rows[0], -1)
    incoming_ids = lax.all_to_all(row_ids, "graph", split_axis=0, concat_axis=0, tiled=True)
    incoming = lax.all_to_all(
        outgoing.reshape(part_count, slot_cap, feat_cols), "graph", split_axis=0, concat_axis=0, tiled=True
    )
    targets = incoming_ids.reshape(-1)
    match = (jnp.arange(node_rows, dtype=jnp.int32)[:, None] == targets[None, :]).astype(jnp.bfloat16)
    neighbor_sum = jnp.dot(match, incoming.reshape(-1, feat_cols), preferred_element_type=jnp.float32)
    degrees = degree.astype(jnp.float32)[:, None]
    neighbor_mean = (neighbor_sum / degrees).astype(jnp.bfloat16)
    agg_full = lax.all_gather(neighbor_mean, "feat", axis=1, tiled=True)
    self_rows = lax.dynamic_slice_in_dim(w_self, column_start, feat_cols, 0)
    neigh_rows = lax.dynamic_slice_in_dim(w_neigh, column_start, feat_cols, 0)
    self_cols = lax.dynamic_slice_in_dim(w_self, column_start, feat_cols, 1)
    neigh_cols = lax.dynamic_slice_in_dim(w_neigh, column_start, feat_cols, 1)
    pre_act = jnp.dot(feat_full, self_cols, preferred_element_type=jnp.float32) + jnp.dot(
        agg_full, neigh_cols, preferred_element_type=jnp.float32
    )
    hidden_out = jax.nn.silu(pre_act).astype(jnp.bfloat16)
    grad_pre = (cotangent.astype(jnp.float32) * silu_slope(pre_act)).astype(jnp.bfloat16)
    grad_full = lax.all_gather(grad_pre, "feat", axis=1, tiled=True)
    local_self = lax.dot_general(
        features, grad_full, (((0,), (0,)), ((), ())), preferred_element_type=jnp.float32
    )
    local_neigh = lax.dot_general(
        neighbor_mean, grad_full, (((0,), (0,)), ((), ())), preferred_element_type=jnp.float32
    )
    grad_self, grad_neigh = lax.psum((local_self, local_neigh), "graph")
    back_rows = (
        lax.dot_general(
            grad_full, neigh_rows, (((1,), (1,)), ((), ())), preferred_element_type=jnp.float32
        )
        / degrees
    ).astype(jnp.bfloat16)
    sending_back = lax.dot_general(
        match, back_rows, (((0,), (0,)), ((), ())), preferred_element_type=jnp.float32
    ).astype(jnp.bfloat16)
    returned = lax.all_to_all(
        sending_back.reshape(part_count, slot_cap, feat_cols), "graph", split_axis=0, concat_axis=0, tiled=True
    )
    grad_features = spread(
        block_source, block_to_slot, adjacency,
        returned.reshape(slot_total, block_size, feat_cols), grad_full, self_rows,
    )
    return (hidden_out, grad_features, grad_self, grad_neigh)


def solution(mesh):
    placed = (
        P("graph", "feat"),
        P(),
        P(),
        P("graph", None, None),
        P("graph"),
        P("graph"),
        P("graph", None, None),
        P("graph", None),
        P("graph"),
        P("graph", "feat"),
    )
    return jax.shard_map(
        on_device,
        mesh=mesh,
        in_specs=placed,
        out_specs=(P("graph", "feat"), P("graph", "feat"), P("feat", None), P("feat", None)),
        check_vma=False,
    )
```

time: 356 us -> 310 us (0.87)
  other arithmetic: 40.2 us -> 1.53 us
  local copies, waits for them, and re-layouts: 34 us -> 12.3 us
  Pallas kernels: 0 us -> 13.2 us
  waiting for transfers between devices: 209 us -> 218 us
  matrix products: 39 us -> 31 us
    reduce_scatter x1 -> x0, waiting for transfers between devices: 68.9 us -> none  [on_device(): lax.psum_scatter(own_term + agg_term, 'feat', scatter_dimension=0, tiled=...]
    all_gather x0 -> x2, waiting for transfers between devices: none -> 64.8 us  [the longest x1 33.1 us: on_device(): agg_full = lax.all_gather(neighbor_mean, 'feat', axis=1, tiled=True)]
    scatter-add x3 -> x0, other arithmetic: 28.6 us -> none  [the longest x1 12.4 us: on_device(): neighbor_sum = jnp.zeros((node_rows, feat_cols), jnp.float32).at[target_r...]
    all_to_all x2, waiting for transfers between devices: 49.8 us -> 64 us  [the longest x1 38.7 us: on_device(): lax.all_to_all(sending_back.reshape(part_count, slot_cap, feat_cols), 'gr...]
    pallas_call x0 -> x2, Pallas kernels: none -> 13.2 us  [the longest x1 9.42 us: spread(): pl.pallas_call(spread_kernel, out_shape=jax.ShapeDtypeStruct((nodes, cols...]
    gather x3 -> x0, local copies, waits for them, and re-layouts: 12.9 us -> none  [the longest x1 7.5 us: on_device(): jnp.take(back_rows, lookup, axis=0)]
    dot_general x2 -> x0, local copies, waits for them, and re-layouts: 11.3 us -> none  [the longest x1 5.65 us: on_device(): jnp.einsum('kij,kid->kjd', adjacency, chosen, preferred_element_type=jnp....]
    dot_general x6 -> x4, matrix products: 31.7 us -> 23.9 us  [the longest x1 8.71 us: on_device(): lax.dot_general(match, back_rows, (((0,), (0,)), ((), ())), preferred_ele...]
  transfers between devices with their start and end apart: 6 -> 7, of which waited for: 5 -> 6; matrix products, arithmetic and copies ran while one was open for 19% -> 5% of each run, Pallas kernels for 0% -> 4%
where the time goes in v1:
time: 310 us
  waiting for transfers between devices  218 us (70%)
  matrix products  31 us (10%)
  starting transfers between devices  19.3 us (6%)
  between operations  13.8 us (4%)
  Pallas kernels  13.2 us (4%)
  local copies, waits for them, and re-layouts  12.3 us (4%)
    psum x1, waiting for transfers between devices, on_device(): grad_self, grad_neigh = lax.psum((local_self, local_neigh), 'graph')  53.8 us
    all_to_all x1, waiting for transfers between devices, on_device(): lax.all_to_all(sending_back.reshape(part_count, slot_cap, feat_cols), 'gr...  38.7 us
    all_gather x1, waiting for transfers between devices, on_device(): grad_full = lax.all_gather(grad_pre, 'feat', axis=1, tiled=True)  34.9 us
    all_gather x1, waiting for transfers between devices, on_device(): agg_full = lax.all_gather(neighbor_mean, 'feat', axis=1, tiled=True)  33.1 us
    all_gather x1, waiting for transfers between devices, on_device(): feat_full = lax.all_gather(features, 'feat', axis=1, tiled=True)  31.7 us
    all_to_all x1, waiting for transfers between devices, on_device(): lax.all_to_all(outgoing.reshape(part_count, slot_cap, feat_cols), 'graph'...  25.4 us
    unnamed x34, local copies, waits for them, and re-layouts  11.4 us
    pallas_call x1, Pallas kernels, spread(): pl.pallas_call(spread_kernel, out_shape=jax.ShapeDtypeStruct((nodes, cols...  9.42 us
  transfers between devices with their start and end apart: 7, of which 6 were waited for; matrix products, arithmetic and copies ran while one was open for 5% of the time, Pallas kernels for 4%

profile of v1, /device:TPU:0, one launch (start us, length us, event | category | flops | bytes accessed | tf_op | source)
XLA Modules:
  0.0 309.5 jit_solution(6024290472802375598)
XLA Ops:
  7.2 0.0 copy-start
  7.2 1.5 compare_select_fusion
  8.7 7.3 %all-to-all-start = ((s32[8,1,256]{2,1,0:T(1,128)}), s32[8,1,256]{2,1,0:T(1,128)S(1)}, u32[]{:S(2)}, u32[]{:S(2)}) async-start(s32[8,1,256]{2,1,0:T(1,128)} %compare_select_fusion), calls=%async_computation | async-start | bytes 16384 | tf_op jit(solution)/shard_map/all_to_all | solution.py:134
  16.0 1.2 copy-done.1
  17.2 1.2 copy-done.5
  18.4 0.7 copy-done.8
  19.1 0.7 copy-done.10
  19.7 0.7 copy-done.12
  20.4 3.8 %collect.1 = bf16[16,128,256]{2,1,0:T(8,128)(2,1)} custom-call(s32[32]{0:T(128)S(1)} %copy-done.8, s32[32]{0:T(128)S(1)} %copy-done.10, s32[1,8]{1,0:T(1,128)S(1)} %copy-done.12, bf16[32,128,128]{2,1,0:T(8,128)(2,1)S(1)} %copy-done.1, bf16[2048,256]{1,0:T(8,128)(2,1)S(1)} %copy-done.5), custom_call_target="tpu_custom_call" | custom-call | tf_op jit(solution)/shard_map/collect/pallas_call | solution.py:50
  24.2 0.0 all-to-all-done
  24.2 6.0 %all-to-all-start.1 = ((bf16[8,256,256]{2,1,0:T(8,128)(2,1)}), bf16[8,256,256]{2,1,0:T(8,128)(2,1)S(1)}, u32[]{:S(2)}, u32[]{:S(2)}) async-start(bf16[8,256,256]{2,1,0:T(8,128)(2,1)} %bitcast.3), calls=%async_computation.1 | async-start | bytes 2097152 | tf_op jit(solution)/shard_map/all_to_all | solution.py:135
  30.2 0.0 all-gather.6.cloned.1.call-start
  30.3 0.0 copy-done.14
  30.3 25.4 %all-to-all-done.1 = bf16[8,256,256]{2,1,0:T(8,128)(2,1)S(1)} async-done(((bf16[8,256,256]{2,1,0:T(8,128)(2,1)}), bf16[8,256,256]{2,1,0:T(8,128)(2,1)S(1)}, u32[]{:S(2)}, u32[]{:S(2)}) %all-to-all-start.1) | async-done | bytes 1048608 | tf_op jit(solution)/shard_map/all_to_all | solution.py:135
  55.7 4.2 %fusion.7 = bf16[2048,256]{1,0:T(8,128)(2,1)} fusion(bf16[2048,256]{1,0:T(8,128)(2,1)S(1)} %bitcast.21, s32[2048]{0:T(1024)S(1)} %bitcast.23, f32[2048]{0:T(1024)S(1)} %convert_element_type.22), kind=kOutput, calls=%fused_computation.9 | convolution fusion | flops 2152726528 | bytes 2113536 | tf_op jit(solution)/shard_map/dot_general | solution.py:140
  59.9 0.0 all-gather.6.cloned.1.call-update
  59.9 0.0 all-gather.4.cloned.1.call-start
  60.0 0.7 all-gather.4.cloned.1.call-update
  60.7 0.0 all-gather.8.cloned.1.call-start
  60.7 0.0 copy-start.15
  60.7 33.1 %all-gather.6.cloned.1.call-done = bf16[2048,1024]{1,0:T(8,128)(2,1)} async-done(((bf16[2048,256]{1,0:T(8,128)(2,1)}), bf16[2048,1024]{1,0:T(8,128)(2,1)}) %all-gather.6.cloned.1.call-update) | async-done | bytes 4194320 | tf_op jit(solution)/shard_map/all_gather | solution.py:143
  93.9 4.9 %fusion.11 = f32[2048,256]{1,0:T(8,128)} fusion(bf16[2048,1024]{1,0:T(8,128)(2,1)} %all-gather.6.cloned.1.call-done, bf16[1024,1024]{1,0:T(8,128)(2,1)} %param.12, s32[]{:T(128)S(6)} %select_n.17), kind=kOutput, calls=%fused_computation.17 | convolution fusion | flops 1073741824 | bytes 6815748 | tf_op jit(solution)/shard_map/dot_general | solution.py:148
  98.8 31.7 %all-gather.4.cloned.1.call-done = bf16[2048,1024]{1,0:T(8,128)(2,1)} async-done(((bf16[2048,256]{1,0:T(8,128)(2,1)}), bf16[2048,1024]{1,0:T(8,128)(2,1)}) %all-gather.4.cloned.1.call-update) | async-done | bytes 4194320 | tf_op jit(solution)/shard_map/all_gather | solution.py:130
  130.5 0.0 copy-done
  130.5 0.0 copy-done.15
  130.5 6.0 %multiply_convert_fusion = (bf16[2048,256]{1,0:T(8,128)(2,1)}, bf16[2048,256]{1,0:T(8,128)(2,1)}) fusion(bf16[2048,256]{1,0:T(8,128)(2,1)S(1)} %copy-done.15, f32[2048,256]{1,0:T(8,128)} %fusion.11, bf16[2048,1024]{1,0:T(8,128)(2,1)} %all-gather.4.cloned.1.call-done, bf16[1024,1024]{1,0:T(8,128)(2,1)S(1)} %copy-done, s32[]{:T(128)S(6)} %select_n.17), kind=kOutput, calls=%fused_computation.12 | convolution fusion | flops 1080557568 | bytes 9961476 | tf_op jit(solution)/shard_map/dot_general | solution.py:148
  136.5 0.0 all-gather.8.cloned.1.call-update
  136.5 0.0 copy-start.6
  136.5 0.2 all-reduce.3.cloned.1.call-start
  136.8 34.9 %all-gather.8.cloned.1.call-done.grad_ref = bf16[2048,1024]{1,0:T(8,128)(2,1)} async-done(((bf16[2048,256]{1,0:T(8,128)(2,1)}), bf16[2048,1024]{1,0:T(8,128)(2,1)}) %all-gather.8.cloned.1.call-update) | async-done | bytes 4194320 | tf_op jit(solution)/shard_map/all_gather | solution.py:153
  171.7 4.9 %fusion.18 = f32[256,1024]{1,0:T(8,128)} fusion(bf16[2048,256]{1,0:T(8,128)(2,1)} %fusion.7, bf16[2048,1024]{1,0:T(8,128)(2,1)} %all-gather.8.cloned.1.call-done.grad_ref), kind=kOutput, calls=%fused_computation.25 | convolution fusion | flops 1073741824 | bytes 6291456 | tf_op jit(solution)/shard_map/dot_general | solution.py:157
  176.6 0.0 copy-done.6
  176.6 0.0 copy-done.3
  176.6 2.3 convolution_bitcast_fusion.1
  178.9 0.0 all-reduce.3.cloned.1.call-update
  178.9 8.7 %fusion.5 = bf16[2048,256]{1,0:T(8,128)(2,1)} fusion(s32[2048]{0:T(1024)S(1)} %bitcast.24, bf16[2048,1024]{1,0:T(8,128)(2,1)} %all-gather.8.cloned.1.call-done.grad_ref, f32[2048]{0:T(1024)S(1)} %convert_element_type.22, bf16[1024,1024]{1,0:T(8,128)(2,1)} %param.12, s32[]{:T(128)S(6)} %select_n.17), kind=kOutput, calls=%fused_computation.7 | convolution fusion | flops 3226992640 | bytes 5783556 | tf_op jit(solution)/shard_map/dot_general | solution.py:167
  187.6 5.6 %all-to-all-start.2 = ((bf16[8,256,256]{2,1,0:T(8,128)(2,1)}), bf16[8,256,256]{2,1,0:T(8,128)(2,1)}, u32[]{:S(2)}, u32[]{:S(2)}) async-start(bf16[8,256,256]{2,1,0:T(8,128)(2,1)} %bitcast.22), calls=%async_computation.2 | async-start | bytes 2097152 | tf_op jit(solution)/shard_map/all_to_all | solution.py:170
  193.3 0.8 constant_dynamic-slice_fusion.w_ref
  194.1 38.7 %all-to-all-done.2 = bf16[8,256,256]{2,1,0:T(8,128)(2,1)} async-done(((bf16[8,256,256]{2,1,0:T(8,128)(2,1)}), bf16[8,256,256]{2,1,0:T(8,128)(2,1)}, u32[]{:S(2)}, u32[]{:S(2)}) %all-to-all-start.2) | async-done | bytes 1048608 | tf_op jit(solution)/shard_map/all_to_all | solution.py:170
  232.8 0.0 copy-done.2
  232.8 0.0 copy-done.9
  232.8 2.4 copy-done.4
  235.2 1.0 copy-done.7
  236.2 9.4 %spread.1 = bf16[2048,256]{1,0:T(8,128)(2,1)} custom-call(s32[32]{0:T(128)S(1)} %copy-done.9, s32[32]{0:T(128)S(1)} %copy-done.11, bf16[32,128,128]{2,1,0:T(8,128)(2,1)S(1)} %copy-done.2, bf16[16,128,256]{2,1,0:T(8,128)(2,1)} %bitcast.6.ret_ref, bf16[2048,1024]{1,0:T(8,128)(2,1)S(1)} %copy-done.4, bf16[256,1024]{1,0:T(8,128)(2,1)S(1)} %copy-done.7), custom_call_target="tpu_custom_call" | custom-call | tf_op jit(solution)/shard_map/spread/pallas_call | solution.py:101
  245.6 53.8 %all-reduce.3.cloned.1.call-done = (f32[256,1024]{0,1:T(8,128)}, f32[256,1024]{1,0:T(8,128)}) async-done(((f32[256,1024]{0,1:T(8,128)}, f32[256,1024]{1,0:T(8,128)}), (f32[256,1024]{0,1:T(8,128)}, f32[256,1024]{1,0:T(8,128)})) %all-reduce.3.cloned.1.call-update) | async-done | bytes 2097168 | tf_op jit(solution)/shard_map/psum | solution.py:160
  299.4 2.6 copy.17
  302.0 0.0 copy-done.13
  302.0 1.0 copy.21
  (15 shorter events, 0.0 us)
Async XLA Ops:
  7.2 123.3 %copy-start = (bf16[1024,1024]{1,0:T(8,128)(2,1)S(1)}, bf16[1024,1024]{1,0:T(8,128)(2,1)}, u32[]{:S(2)}) copy-start(bf16[1024,1024]{1,0:T(8,128)(2,1)} %param.11) | copy-start | bytes 6291460
  8.7 15.5 %all-to-all-start = ((s32[8,1,256]{2,1,0:T(1,128)}), s32[8,1,256]{2,1,0:T(1,128)S(1)}, u32[]{:S(2)}, u32[]{:S(2)}) async-start(s32[8,1,256]{2,1,0:T(1,128)} %compare_select_fusion), calls=%async_computation | async-start | bytes 16384 | tf_op jit(solution)/shard_map/all_to_all | solution.py:134
  16.0 1.2 copy-start.1
  17.2 1.2 copy-start.5
  18.4 0.7 copy-start.8
  19.1 0.7 copy-start.10
  19.7 0.7 copy-start.12
  20.4 9.9 %copy-start.14 = (s32[2048]{0:T(1024)S(1)}, s32[2048]{0:T(1024)}, u32[]{:S(2)}) copy-start(s32[2048]{0:T(1024)} %param.18) | copy-start | bytes 24580
  24.2 31.4 %all-to-all-start.1 = ((bf16[8,256,256]{2,1,0:T(8,128)(2,1)}), bf16[8,256,256]{2,1,0:T(8,128)(2,1)S(1)}, u32[]{:S(2)}, u32[]{:S(2)}) async-start(bf16[8,256,256]{2,1,0:T(8,128)(2,1)} %bitcast.3), calls=%async_computation.1 | async-start | bytes 2097152 | tf_op jit(solution)/shard_map/all_to_all | solution.py:135
  30.2 63.6 %all-gather.6.cloned.1.call-start = ((), (), s32[]{:S(2)}) async-start(), calls=%async_computation.4 | async-start | bytes 5242880 | tf_op jit(solution)/shard_map/all_gather | solution.py:143
  59.9 70.6 %all-gather.4.cloned.1.call-start = ((), (), s32[]{:S(2)}) async-start(), calls=%async_computation.3 | async-start | bytes 5242880 | tf_op jit(solution)/shard_map/all_gather | solution.py:130
  60.7 111.1 %all-gather.8.cloned.1.call-start = ((), (), s32[]{:S(2)}) async-start(), calls=%async_computation.5 | async-start | bytes 5242880 | tf_op jit(solution)/shard_map/all_gather | solution.py:153
  60.7 69.8 %copy-start.15 = (bf16[2048,256]{1,0:T(8,128)(2,1)S(1)}, bf16[2048,256]{1,0:T(8,128)(2,1)}, u32[]{:S(2)}) copy-start(bf16[2048,256]{1,0:T(8,128)(2,1)} %param.19) | copy-start | bytes 3145732
  136.5 40.1 %copy-start.6 = (bf16[2048,256]{1,0:T(8,128)(2,1)S(1)}, bf16[2048,256]{1,0:T(8,128)(2,1)}, u32[]{:S(2)}) copy-start(bf16[2048,256]{1,0:T(8,128)(2,1)} %feat_ref.1) | copy-start | bytes 3145732
  136.5 162.8 %all-reduce.3.cloned.1.call-start = ((), (), s32[]{:S(2)}) async-start(), calls=%async_computation.6 | async-start | bytes 4194304 | tf_op jit(solution)/shard_map/psum | solution.py:160
  171.7 4.9 %copy-start.3 = (bf16[2048,1024]{1,0:T(8,128)(2,1)S(1)}, bf16[2048,1024]{1,0:T(8,128)(2,1)}, u32[]{:S(2)}) copy-start(bf16[2048,1024]{1,0:T(8,128)(2,1)} %all-gather.8.cloned.1.call-done.grad_ref) | copy-start | bytes 12582916
  187.6 45.1 %copy-start.2 = (bf16[32,128,128]{2,1,0:T(8,128)(2,1)S(1)}, bf16[32,128,128]{2,1,0:T(8,128)(2,1)}, u32[]{:S(2)}) copy-start(bf16[32,128,128]{2,1,0:T(8,128)(2,1)} %adj_ref.3) | copy-start | bytes 3145732
  187.6 45.1 %copy-start.9 = (s32[32]{0:T(128)S(1)}, s32[32]{0:T(128)}, u32[]{:S(2)}) copy-start(s32[32]{0:T(128)} %source_ref.3) | copy-start | bytes 388
  187.6 45.1 %copy-start.11 = (s32[32]{0:T(128)S(1)}, s32[32]{0:T(128)}, u32[]{:S(2)}) copy-start(s32[32]{0:T(128)} %slot_ref.3) | copy-start | bytes 388
  187.6 45.1 %all-to-all-start.2 = ((bf16[8,256,256]{2,1,0:T(8,128)(2,1)}), bf16[8,256,256]{2,1,0:T(8,128)(2,1)}, u32[]{:S(2)}, u32[]{:S(2)}) async-start(bf16[8,256,256]{2,1,0:T(8,128)(2,1)} %bitcast.22), calls=%async_computation.2 | async-start | bytes 2097152 | tf_op jit(solution)/shard_map/all_to_all | solution.py:170
  232.8 2.4 copy-start.4
  235.2 1.0 copy-start.7
  299.4 2.6 copy-start.13
Sparse Core Ops, SparseCore 0:
  60.0 33.7 all-gather.5
  95.4 35.0 all-gather.3
  136.7 35.0 all-gather.7
  179.0 120.3 all-reduce.2

commit v2 on v1

v2 whole, which is shorter than its diff:
```python
import functools

import jax
import jax.numpy as jnp
from jax import lax
from jax.experimental import pallas as pl
from jax.experimental.pallas import tpu as pltpu
from jax.sharding import PartitionSpec as P

SMEM = pltpu.SMEM
VMEM = pltpu.VMEM
MESH = pl.DeviceIdType.MESH
GROUP = 4
CHUNKS = 4


def collect_kernel(source_ref, slot_ref, count_ref, adj_ref, feat_ref, out_ref, acc):
    blocks, block, _ = adj_ref.shape
    slot_total = out_ref.shape[0]
    halves = slot_total // count_ref.shape[1]
    acc[...] = jnp.zeros_like(acc)

    def add(step, carry):
        prods = []
        for j in range(GROUP):
            k = step * GROUP + j
            rows = pl.ds(pl.multiple_of(source_ref[k] * block, block), block)
            prods.append(jnp.dot(adj_ref[k], feat_ref[rows, :], preferred_element_type=jnp.float32))
        for j in range(GROUP):
            acc[slot_ref[step * GROUP + j]] += prods[j]
        return carry

    lax.fori_loop(0, blocks // GROUP, add, 0)

    def finish(s, carry):
        limit = count_ref[0, s // halves] - (s % halves) * block
        rows = lax.broadcasted_iota(jnp.int32, out_ref.shape[1:], 0)
        out_ref[s] = jnp.where(rows < limit, acc[s], 0.0).astype(jnp.bfloat16)
        return carry

    lax.fori_loop(0, slot_total, finish, 0)


def collect(block_source, block_to_slot, send_counts, adjacency, features, slot_total):
    blocks, block, _ = adjacency.shape
    shape = (slot_total, block, features.shape[1])
    return pl.pallas_call(
        collect_kernel,
        out_shape=jax.ShapeDtypeStruct(shape, jnp.bfloat16),
        in_specs=[pl.BlockSpec(memory_space=SMEM)] * 3 + [pl.BlockSpec(memory_space=VMEM)] * 2,
        out_specs=pl.BlockSpec(memory_space=VMEM),
        scratch_shapes=[pltpu.VMEM(shape, jnp.float32)],
        compiler_params=pltpu.CompilerParams(vmem_limit_bytes=32 * 2**20),
        name="collect",
    )(block_source, block_to_slot, send_counts, adjacency, features)


def spread_kernel(source_ref, slot_ref, adj_ref, ret_ref, start_ref, out_ref, acc):
    blocks, block, _ = adj_ref.shape
    sources = out_ref.shape[0] // block
    acc[...] = start_ref[...]

    def add(step, carry):
        prods = []
        for j in range(GROUP):
            k = step * GROUP + j
            prods.append(lax.dot_general(
                adj_ref[k], ret_ref[slot_ref[k]], (((0,), (0,)), ((), ())),
                preferred_element_type=jnp.float32,
            ))
        for j in range(GROUP):
            acc[source_ref[step * GROUP + j]] += prods[j]
        return carry

    lax.fori_loop(0, blocks // GROUP, add, 0)

    def finish(b, carry):
        rows = pl.ds(pl.multiple_of(b * block, block), block)
        out_ref[rows, :] = acc[b].astype(jnp.bfloat16)
        return carry

    lax.fori_loop(0, sources, finish, 0)


def spread(block_source, block_to_slot, adjacency, returned, self_grad):
    blocks, block, _ = adjacency.shape
    nodes, cols = self_grad.shape
    shape = (nodes // block, block, cols)
    return pl.pallas_call(
        spread_kernel,
        out_shape=jax.ShapeDtypeStruct((nodes, cols), jnp.bfloat16),
        in_specs=[pl.BlockSpec(memory_space=SMEM)] * 2 + [pl.BlockSpec(memory_space=VMEM)] * 3,
        out_specs=pl.BlockSpec(memory_space=VMEM),
        scratch_shapes=[pltpu.VMEM(shape, jnp.float32)],
        compiler_params=pltpu.CompilerParams(vmem_limit_bytes=32 * 2**20),
        name="spread",
    )(block_source, block_to_slot, adjacency, returned, self_grad.reshape(shape))


def layer_kernel(
    parts, feats,
    out_blocks, out_ids, feat_ref, deg_ref, cot_ref, w_self, w_neigh,
    hidden_ref, returned_ref, self_grad_ref, grad_self_ref, grad_neigh_ref,
    in_blocks, in_ids, sum_ref, pre_ref, feat_full, agg_full, grad_full, back_ref, back_out, back_in,
    self_cols, neigh_cols, self_rows, neigh_rows, weight_acc,
    y_out, y_in, z_out, z_in, z_all, y_all,
    a_send, a_recv, i_send, i_recv, r_send, r_recv, w_sem,
    gx_send, gs_send, gr_send, g_recv,
    ys_send, ys_recv, zs_send, zs_recv, za_send, za_recv, ya_send, ya_recv,
):
    g, f = lax.axis_index("graph"), lax.axis_index("feat")
    chips = feats // 2
    ys = chips
    zs = parts // ys
    x, core = f // 2, f % 2
    sibling = x * 2 + 1 - core
    z, y = g // ys, g % ys
    nodes, cols = feat_ref.shape
    width = feats * cols
    chunk = nodes // CHUNKS

    def remote(src, dst, send, recv, graph_to, feat_to):
        return pltpu.make_async_remote_copy(
            src_ref=src, dst_ref=dst, send_sem=send, recv_sem=recv,
            device_id=(graph_to, feat_to), device_id_type=MESH,
        )

    def span(c):
        return pl.ds(pl.multiple_of(c * chunk, chunk), chunk)

    def loop(low, high, body):
        def step(i, carry):
            body(i)
            return carry

        lax.fori_loop(low, high, step, 0)

    def dot(a, b):
        return jnp.dot(a, b, preferred_element_type=jnp.float32)

    def dot_rows(a, b):
        return lax.dot_general(a, b, (((0,), (0,)), ((), ())), preferred_element_type=jnp.float32)

    def dot_cols(a, b):
        return lax.dot_general(a, b, (((1,), (1,)), ((), ())), preferred_element_type=jnp.float32)

    mine = pl.ds(pl.multiple_of(f * cols, cols), cols)
    weights = [
        pltpu.make_async_copy(w_self.at[:, mine], self_cols, w_sem.at[0]),
        pltpu.make_async_copy(w_neigh.at[:, mine], neigh_cols, w_sem.at[1]),
        pltpu.make_async_copy(w_self.at[mine, :], self_rows, w_sem.at[2]),
        pltpu.make_async_copy(w_neigh.at[mine, :], neigh_rows, w_sem.at[3]),
    ]
    for w in weights:
        w.start()

    barrier = pltpu.get_barrier_semaphore()
    for d in range(1, parts):
        pl.semaphore_signal(barrier, inc=1, device_id=((g + d) % parts, f), device_id_type=MESH)
    for d in range(1, feats):
        pl.semaphore_signal(barrier, inc=1, device_id=(g, (f + d) % feats), device_id_type=MESH)
    pl.semaphore_wait(barrier, parts + feats - 2)

    def id_copy(slot, p):
        return remote(out_ids.at[p], in_ids.at[slot], i_send.at[p], i_recv.at[slot], p, f)

    def block_copy(slot, p):
        return remote(out_blocks.at[p], in_blocks.at[slot], a_send.at[p], a_recv.at[slot], p, f)

    def return_copy(slot, p):
        return remote(back_out.at[p], back_in.at[slot], r_send.at[p], r_recv.at[slot], p, f)

    def send_blocks(d):
        p = (g + d) % parts
        id_copy(g, p).start()
        block_copy(g, p).start()

    loop(1, parts, send_blocks)

    def to_sibling(n, full, c):
        piece = full.at[f, span(c)]
        return remote(piece, piece, gs_send.at[n, c], g_recv.at[n, f, c], g, sibling)

    def to_chip(n, full, c, d):
        piece = full.at[f, span(c)]
        return remote(piece, piece, gx_send.at[n, d - 1, c], g_recv.at[n, f, c], g, (x + d) % chips * 2 + core)

    def relay(n, full, c, d):
        j = (x + d) % chips * 2 + core
        piece = full.at[j, span(c)]
        return remote(piece, piece, gr_send.at[n, d - 1, c], g_recv.at[n, j, c], g, sibling)

    def arrival(n, full, c, j):
        piece = full.at[j, span(c)]
        return remote(piece, piece, gs_send.at[n, c], g_recv.at[n, j, c], g, sibling)

    def gather_start(n, full, c):
        for d in range(1, chips):
            to_chip(n, full, c, d).start()
        to_sibling(n, full, c).start()

    def gather_relay(n, full, c):
        for d in range(1, chips):
            arrival(n, full, c, (x + d) % chips * 2 + core).wait_recv()
            relay(n, full, c, d).start()

    def gather_finish(n, full, c):
        arrival(n, full, c, sibling).wait_recv()
        for d in range(1, chips):
            arrival(n, full, c, (x + d) % chips * 2 + 1 - core).wait_recv()

    def gather_sent(n, full, c):
        to_sibling(n, full, c).wait_send()
        for d in range(1, chips):
            to_chip(n, full, c, d).wait_send()
            relay(n, full, c, d).wait_send()

    def feat_start(c):
        feat_full[f, span(c), :] = feat_ref[span(c), :]
        gather_start(0, feat_full, c)

    loop(0, CHUNKS, feat_start)

    cap = out_blocks.shape[1]

    def scatter(ids, values, first):
        def tile(c):
            node = lax.broadcasted_iota(jnp.int32, (chunk, cap), 0) + c * chunk
            match = jnp.where(node == ids, 1.0, 0.0).astype(jnp.bfloat16)
            added = dot(match, values)
            if first:
                sum_ref[span(c), :] = added
            else:
                sum_ref[span(c), :] += added

        loop(0, CHUNKS, tile)

    scatter(out_ids[g][0:1, :], out_blocks[g], True)
    in_ids[g] = out_ids[g]

    def take_blocks(d):
        p = (g + parts - d) % parts
        id_copy(p, p).wait_recv()
        block_copy(p, p).wait_recv()
        scatter(in_ids[p][0:1, :], in_blocks[p], False)

    loop(1, parts, take_blocks)

    def aggregate(c):
        agg_full[f, span(c), :] = (sum_ref[span(c), :] / deg_ref[span(c), :]).astype(jnp.bfloat16)
        gather_start(1, agg_full, c)

    loop(0, CHUNKS, aggregate)
    loop(0, CHUNKS, lambda c: gather_relay(0, feat_full, c))
    for w in weights:
        w.wait()

    def own_term(c):
        gather_finish(0, feat_full, c)
        total = dot(feat_full[0, span(c), :], self_cols[0:cols, :])
        for j in range(1, feats):
            total += dot(feat_full[j, span(c), :], self_cols[j * cols:(j + 1) * cols, :])
        pre_ref[span(c), :] = total

    loop(0, CHUNKS, own_term)

    def activate(c):
        gather_relay(1, agg_full, c)
        gather_finish(1, agg_full, c)
        total = pre_ref[span(c), :]
        for j in range(feats):
            total += dot(agg_full[j, span(c), :], neigh_cols[j * cols:(j + 1) * cols, :])
        sig = jax.nn.sigmoid(total)
        hidden_ref[span(c), :] = (total * sig).astype(jnp.bfloat16)
        slope = sig * (1.0 + total * (1.0 - sig))
        grad_full[f, span(c), :] = (cot_ref[span(c), :].astype(jnp.float32) * slope).astype(jnp.bfloat16)
        gather_start(2, grad_full, c)

    loop(0, CHUNKS, activate)

    def weight_grads(c):
        for j in range(feats):
            at = slice(j * cols, (j + 1) * cols)
            weight_acc[0:cols, at] += dot_rows(feat_ref[span(c), :], grad_full[j, span(c), :])
            weight_acc[cols:2 * cols, at] += dot_rows(agg_full[f, span(c), :], grad_full[j, span(c), :])

    def back_rows(c):
        gather_relay(2, grad_full, c)
        gather_finish(2, grad_full, c)
        total = dot_cols(grad_full[0, span(c), :], neigh_rows[:, 0:cols])
        for j in range(1, feats):
            total += dot_cols(grad_full[j, span(c), :], neigh_rows[:, j * cols:(j + 1) * cols])
        back_ref[span(c), :] = (total / deg_ref[span(c), :]).astype(jnp.bfloat16)

    weight_acc[...] = jnp.zeros_like(weight_acc)

    def backward(c):
        back_rows(c)
        weight_grads(c)

    loop(0, CHUNKS - 1, backward)
    back_rows(CHUNKS - 1)

    def pick(p):
        ids = jnp.transpose(in_ids[p])[:, 0:1]
        total = jnp.zeros((cap, cols), jnp.float32)
        for c in range(CHUNKS):
            node = lax.broadcasted_iota(jnp.int32, (cap, chunk), 1) + c * chunk
            match = jnp.where(node == ids, 1.0, 0.0).astype(jnp.bfloat16)
            total += dot(match, back_ref[c * chunk:(c + 1) * chunk, :])
        return total.astype(jnp.bfloat16)

    def send_back(d):
        p = (g + d) % parts
        back_out[p] = pick(p)
        return_copy(g, p).start()

    loop(1, parts, send_back)
    back_in[g] = pick(g)
    weight_grads(CHUNKS - 1)

    tall, wide = 2 * cols // ys, width // zs
    for a in range(ys):
        for b in range(zs):
            y_out[a, b] = weight_acc[a * tall:(a + 1) * tall, b * wide:(b + 1) * wide].astype(jnp.bfloat16)

    def y_copy(slot, to):
        return remote(y_out.at[to], y_in.at[slot], ys_send.at[to], ys_recv.at[slot], z * ys + to, f)

    def z_copy(slot, to):
        return remote(z_out.at[to], z_in.at[slot], zs_send.at[to], zs_recv.at[slot], to * ys + y, f)

    def z_gather(slot, to):
        return remote(z_all.at[slot], z_all.at[slot], za_send.at[to], za_recv.at[slot], to * ys + y, f)

    def y_gather(slot, to):
        return remote(y_all.at[slot], y_all.at[slot], ya_send.at[to], ya_recv.at[slot], z * ys + to, f)

    for d in range(1, ys):
        y_copy(y, (y + d) % ys).start()

    def self_part(c):
        total = dot_cols(grad_full[0, span(c), :], self_rows[:, 0:cols])
        for j in range(1, feats):
            total += dot_cols(grad_full[j, span(c), :], self_rows[:, j * cols:(j + 1) * cols])
        self_grad_ref[span(c), :] = total

    loop(0, CHUNKS, self_part)
    y_in[y] = y_out[y]
    for d in range(1, ys):
        p = (y + d) % ys
        y_copy(p, p).wait_recv()
    for b in range(zs):
        total = y_in[0, b].astype(jnp.float32)
        for a in range(1, ys):
            total += y_in[a, b].astype(jnp.float32)
        z_out[b] = total.astype(jnp.bfloat16)
    for d in range(1, zs):
        z_copy(z, (z + d) % zs).start()
    z_in[z] = z_out[z]
    for d in range(1, zs):
        p = (z + d) % zs
        z_copy(p, p).wait_recv()
    total = z_in[0].astype(jnp.float32)
    for b in range(1, zs):
        total += z_in[b].astype(jnp.float32)
    z_all[z] = total.astype(jnp.bfloat16)
    for d in range(1, zs):
        z_gather(z, (z + d) % zs).start()
    for d in range(1, zs):
        p = (z + d) % zs
        z_gather(p, p).wait_recv()
    y_all[y] = z_all[...]
    for d in range(1, ys):
        y_gather(y, (y + d) % ys).start()

    def returned(d):
        p = (g + parts - d) % parts
        return_copy(p, p).wait_recv()
        returned_ref[p] = back_in[p]

    returned_ref[g] = back_in[g]
    loop(1, parts, returned)

    for d in range(1, ys):
        p = (y + d) % ys
        y_gather(p, p).wait_recv()
    for a in range(ys):
        for b in range(zs):
            piece = y_all[a, b].astype(jnp.float32)
            at = slice(b * wide, (b + 1) * wide)
            if a < ys // 2:
                grad_self_ref[a * tall:(a + 1) * tall, at] = piece
            else:
                low = a - ys // 2
                grad_neigh_ref[low * tall:(low + 1) * tall, at] = piece

    def sent(d):
        p = (g + d) % parts
        id_copy(g, p).wait_send()
        block_copy(g, p).wait_send()
        return_copy(g, p).wait_send()

    loop(1, parts, sent)
    for n, full in enumerate((feat_full, agg_full, grad_full)):
        loop(0, CHUNKS, functools.partial(gather_sent, n, full))
    for d in range(1, ys):
        y_copy(y, (y + d) % ys).wait_send()
        y_gather(y, (y + d) % ys).wait_send()
    for d in range(1, zs):
        z_copy(z, (z + d) % zs).wait_send()
        z_gather(z, (z + d) % zs).wait_send()


def layer(outgoing, row_ids, features, degrees, cotangent, w_self, w_neigh):
    parts, cap, cols = outgoing.shape
    nodes = features.shape[0]
    feats = lax.axis_size("feat")
    width = feats * cols
    ys = feats // 2
    zs = parts // ys
    tall, wide = 2 * cols // ys, width // zs
    bf16, f32 = jnp.bfloat16, jnp.float32
    dma = pltpu.SemaphoreType.DMA
    hops = max(feats // 2 - 1, 1)
    return pl.pallas_call(
        functools.partial(layer_kernel, parts, feats),
        out_shape=(
            jax.ShapeDtypeStruct((nodes, cols), bf16),
            jax.ShapeDtypeStruct((parts, cap, cols), bf16),
            jax.ShapeDtypeStruct((nodes, cols), f32),
            jax.ShapeDtypeStruct((cols, width), f32),
            jax.ShapeDtypeStruct((cols, width), f32),
        ),
        in_specs=[pl.BlockSpec(memory_space=VMEM)] * 5 + [pl.BlockSpec(memory_space=pl.ANY)] * 2,
        out_specs=[pl.BlockSpec(memory_space=VMEM)] * 5,
        scratch_shapes=[
            pltpu.VMEM((parts, cap, cols), bf16),
            pltpu.VMEM(row_ids.shape, jnp.int32),
            pltpu.VMEM((nodes, cols), f32),
            pltpu.VMEM((nodes, cols), f32),
            pltpu.VMEM((feats, nodes, cols), bf16),
            pltpu.VMEM((feats, nodes, cols), bf16),
            pltpu.VMEM((feats, nodes, cols), bf16),
            pltpu.VMEM((nodes, cols), bf16),
            pltpu.VMEM((parts, cap, cols), bf16),
            pltpu.VMEM((parts, cap, cols), bf16),
            pltpu.VMEM((width, cols), bf16),
            pltpu.VMEM((width, cols), bf16),
            pltpu.VMEM((cols, width), bf16),
            pltpu.VMEM((cols, width), bf16),
            pltpu.VMEM((2 * cols, width), f32),
            pltpu.VMEM((ys, zs, tall, wide), bf16),
            pltpu.VMEM((ys, zs, tall, wide), bf16),
            pltpu.VMEM((zs, tall, wide), bf16),
            pltpu.VMEM((zs, tall, wide), bf16),
            pltpu.VMEM((zs, tall, wide), bf16),
            pltpu.VMEM((ys, zs, tall, wide), bf16),
            dma((parts,)), dma((parts,)), dma((parts,)), dma((parts,)), dma((parts,)), dma((parts,)),
            dma((4,)),
            dma((3, hops, CHUNKS)), dma((3, CHUNKS)), dma((3, hops, CHUNKS)), dma((3, feats, CHUNKS)),
            dma((ys,)), dma((ys,)), dma((zs,)), dma((zs,)), dma((zs,)), dma((zs,)), dma((ys,)), dma((ys,)),
        ],
        compiler_params=pltpu.CompilerParams(
            collective_id=0, has_side_effects=True, vmem_limit_bytes=56 * 2**20
        ),
        name="layer",
    )(outgoing, row_ids, features, degrees, cotangent, w_self, w_neigh)


def on_device(
    features,
    w_self,
    w_neigh,
    adjacency,
    block_source,
    block_to_slot,
    send_rows,
    send_counts,
    degree,
    cotangent,
):
    part_count = lax.axis_size("graph")
    feat_cols = features.shape[1]
    block_size = adjacency.shape[1]
    slot_cap = send_rows.shape[2]
    slot_total = part_count * slot_cap // block_size
    outgoing = collect(block_source, block_to_slot, send_counts, adjacency, features, slot_total)
    is_live = jnp.arange(slot_cap, dtype=jnp.int32)[None, :] < send_counts[0][:, None]
    row_ids = jnp.where(is_live, send_rows[0], -1)
    row_ids = jnp.broadcast_to(row_ids[:, None, :], (part_count, 8, slot_cap))
    degrees = degree.astype(jnp.float32)[:, None]
    hidden_out, returned, self_grad, grad_self, grad_neigh = layer(
        outgoing.reshape(part_count, slot_cap, feat_cols), row_ids, features, degrees, cotangent, w_self, w_neigh
    )
    grad_features = spread(
        block_source, block_to_slot, adjacency,
        returned.reshape(slot_total, block_size, feat_cols), self_grad,
    )
    return (hidden_out, grad_features, grad_self, grad_neigh)


def solution(mesh):
    placed = (
        P("graph", "feat"),
        P(),
        P(),
        P("graph", None, None),
        P("graph"),
        P("graph"),
        P("graph", None, None),
        P("graph", None),
        P("graph"),
        P("graph", "feat"),
    )
    return jax.shard_map(
        on_device,
        mesh=mesh,
        in_specs=placed,
        out_specs=(P("graph", "feat"), P("graph", "feat"), P("feat", None), P("feat", None)),
        check_vma=False,
    )
```

time: 310 us -> 174 us (0.56)
  waiting for transfers between devices: 218 us -> 0 us
  Pallas kernels: 13.2 us -> 155 us
  matrix products: 31 us -> 0 us
  starting transfers between devices: 19.3 us -> 0 us
  between operations: 13.8 us -> 0.7 us
    pallas_call x0 -> x1, Pallas kernels: none -> 148 us  [layer(): pl.pallas_call(functools.partial(layer_kernel, parts, feats), out_shape=(...]
    all_gather x3 -> x0, waiting for transfers between devices: 99.8 us -> none  [the longest x1 34.9 us: on_device(): grad_full = lax.all_gather(grad_pre, 'feat', axis=1, tiled=True)]
    all_to_all x3 -> x0, waiting for transfers between devices: 64 us -> none  [the longest x1 38.7 us: on_device(): lax.all_to_all(sending_back.reshape(part_count, slot_cap, feat_cols), 'gr...]
    psum x1 -> x0, waiting for transfers between devices: 53.8 us -> none  [on_device(): grad_self, grad_neigh = lax.psum((local_self, local_neigh), 'graph')]
    dot_general x6 -> x0, matrix products: 31 us -> none  [the longest x1 8.71 us: on_device(): lax.dot_general(match, back_rows, (((0,), (0,)), ((), ())), preferred_ele...]
    all_to_all x3 -> x0, starting transfers between devices: 18.9 us -> none  [the longest x1 7.28 us: on_device(): lax.all_to_all(row_ids, 'graph', split_axis=0, concat_axis=0, tiled=True)]
    pallas_call x1, Pallas kernels: 9.42 us -> 3.98 us  [spread(): pl.pallas_call(spread_kernel, out_shape=jax.ShapeDtypeStruct((nodes, cols...]
    unnamed x34 -> x31, local copies, waits for them, and re-layouts: 11.4 us -> 11.7 us
  transfers between devices with their start and end apart: 7 -> 0, of which waited for: 6 -> 0; matrix products, arithmetic and copies ran while one was open for 5% -> 0% of each run, Pallas kernels for 4% -> 0%
where the time goes in v2:
time: 174 us; the launch traced here: 171 us
  Pallas kernels  155 us (89%)
  local copies, waits for them, and re-layouts  13.7 us (8%)
    pallas_call x1, Pallas kernels, layer(): pl.pallas_call(functools.partial(layer_kernel, parts, feats), out_shape=(...  148 us
    unnamed x31, local copies, waits for them, and re-layouts  11.7 us
    pallas_call x1, Pallas kernels, spread(): pl.pallas_call(spread_kernel, out_shape=jax.ShapeDtypeStruct((nodes, cols...  3.98 us

profile of v2, /device:TPU:0, one launch (start us, length us, event | category | flops | bytes accessed | tf_op | source)
XLA Modules:
  0.0 171.0 jit_solution(4009579555427820490)
XLA Ops:
  0.6 0.8 bitcast_select_fusion
  1.4 0.7 convert_element_type.3
  2.1 0.6 broadcast_in_dim.15.out_ids
  2.7 1.3 copy.14.deg_ref
  4.1 0.0 copy-start
  4.1 1.2 copy-done
  5.3 0.0 copy-start.2
  5.3 1.2 copy-done.2
  6.5 0.0 copy-start.6
  6.5 0.7 copy-done.6
  7.2 0.0 copy-start.8
  7.2 0.7 copy-done.8
  7.8 0.0 copy-start.10
  7.8 0.7 copy-done.10
  8.5 2.8 %collect.1 = bf16[16,128,256]{2,1,0:T(8,128)(2,1)S(1)} custom-call(s32[32]{0:T(128)S(1)} %copy-done.6, s32[32]{0:T(128)S(1)} %copy-done.8, s32[1,8]{1,0:T(1,128)S(1)} %copy-done.10, bf16[32,128,128]{2,1,0:T(8,128)(2,1)S(1)} %copy-done, bf16[2048,256]{1,0:T(8,128)(2,1)S(1)} %copy-done.2), custom_call_target="tpu_custom_call" | custom-call | tf_op jit(solution)/shard_map/collect/pallas_call | solution.py:47
  11.4 0.0 copy-start.3
  11.4 1.0 copy-done.3
  12.3 0.0 copy-start.1
  12.3 0.0 copy-start.7
  12.3 0.0 copy-start.9
  12.3 148.3 %layer.1 = (bf16[2048,256]{1,0:T(8,128)(2,1)}, bf16[8,256,256]{2,1,0:T(8,128)(2,1)}, f32[2048,256]{1,0:T(8,128)}, f32[256,1024]{1,0:T(8,128)}, f32[256,1024]{1,0:T(8,128)}) custom-call(bf16[8,256,256]{2,1,0:T(8,128)(2,1)} %bitcast.7, s32[8,8,256]{2,1,0:T(8,128)} %broadcast_in_dim.15.out_ids, bf16[2048,256]{1,0:T(8,128)(2,1)} %feat_ref.3, ...), custom_call_target="tpu_custom_call" | custom-call | tf_op jit(solution)/shard_map/layer/pallas_call | solution.py:426
  160.6 0.0 copy-done.1
  160.6 0.0 copy-done.7
  160.7 0.0 copy-done.9
  160.7 0.0 copy-start.4
  160.7 1.6 copy-done.4
  162.3 0.0 copy-start.5
  162.3 1.2 copy-done.5
  163.5 0.0 copy-start.13
  163.5 4.0 %spread.1 = bf16[2048,256]{1,0:T(8,128)(2,1)} custom-call(s32[32]{0:T(128)S(1)} %copy-done.7, s32[32]{0:T(128)S(1)} %copy-done.9, bf16[32,128,128]{2,1,0:T(8,128)(2,1)S(1)} %copy-done.1, bf16[16,128,256]{2,1,0:T(8,128)(2,1)S(1)} %bitcast.9, f32[16,128,256]{2,1,0:T(8,128)S(1)} %bitcast.8), custom_call_target="tpu_custom_call" | custom-call | tf_op jit(solution)/shard_map/spread/pallas_call | solution.py:89
  167.5 0.0 copy-done.13
  167.5 0.0 copy-start.12
  167.5 0.0 copy-start.11
  167.5 1.0 copy.18
  168.4 0.6 copy-done.12
  169.1 1.0 copy.19
  170.0 0.0 copy-done.11
  170.0 1.0 copy.20
Async XLA Ops:
  4.1 1.2 copy-start
  5.3 1.2 copy-start.2
  6.5 0.7 copy-start.6
  7.2 0.7 copy-start.8
  7.8 0.7 copy-start.10
  11.4 1.0 copy-start.3
  12.3 148.3 %copy-start.1 = (bf16[32,128,128]{2,1,0:T(8,128)(2,1)S(1)}, bf16[32,128,128]{2,1,0:T(8,128)(2,1)}, u32[]{:S(2)}) copy-start(bf16[32,128,128]{2,1,0:T(8,128)(2,1)} %adj_ref.3) | copy-start | bytes 3145732
  12.3 148.3 %copy-start.7 = (s32[32]{0:T(128)S(1)}, s32[32]{0:T(128)}, u32[]{:S(2)}) copy-start(s32[32]{0:T(128)} %source_ref.3) | copy-start | bytes 388
  12.3 148.3 %copy-start.9 = (s32[32]{0:T(128)S(1)}, s32[32]{0:T(128)}, u32[]{:S(2)}) copy-start(s32[32]{0:T(128)} %slot_ref.3) | copy-start | bytes 388
  160.7 1.6 copy-start.4
  162.3 1.2 copy-start.5
  163.5 4.0 %copy-start.13 = (bf16[2048,256]{1,0:T(8,128)(2,1)S(1)}, bf16[2048,256]{1,0:T(8,128)(2,1)}, u32[]{:S(2)}) copy-start(bf16[2048,256]{1,0:T(8,128)(2,1)} %get-tuple-element.18) | copy-start | bytes 3145732
  167.5 1.6 copy-start.12
  167.5 2.6 %copy-start.11 = (f32[256,1024]{1,0:T(8,128)S(1)}, f32[256,1024]{1,0:T(8,128)}, u32[]{:S(2)}) copy-start(f32[256,1024]{1,0:T(8,128)} %get-tuple-element.21) | copy-start | bytes 3145732

commit v3 on v2

--- a/solution.py
+++ b/solution.py
@@ -14,11 +14,17 @@
 CHUNKS = 4
 
 
-def collect_kernel(source_ref, slot_ref, count_ref, adj_ref, feat_ref, out_ref, acc):
+def collect_kernel(source_ref, slot_ref, count_ref, adj_hbm, feat_hbm, out_ref, acc, adj_ref, feat_ref, sems):
+    adj_copy = pltpu.make_async_copy(adj_hbm, adj_ref, sems.at[0])
+    feat_copy = pltpu.make_async_copy(feat_hbm, feat_ref, sems.at[1])
+    adj_copy.start()
+    feat_copy.start()
     blocks, block, _ = adj_ref.shape
     slot_total = out_ref.shape[0]
     halves = slot_total // count_ref.shape[1]
     acc[...] = jnp.zeros_like(acc)
+    adj_copy.wait()
+    feat_copy.wait()
 
     def add(step, carry):
         prods = []
@@ -47,18 +53,39 @@
     return pl.pallas_call(
         collect_kernel,
         out_shape=jax.ShapeDtypeStruct(shape, jnp.bfloat16),
-        in_specs=[pl.BlockSpec(memory_space=SMEM)] * 3 + [pl.BlockSpec(memory_space=VMEM)] * 2,
+        in_specs=[pl.BlockSpec(memory_space=SMEM)] * 3 + [pl.BlockSpec(memory_space=pl.ANY)] * 2,
         out_specs=pl.BlockSpec(memory_space=VMEM),
-        scratch_shapes=[pltpu.VMEM(shape, jnp.float32)],
+        scratch_shapes=[
+            pltpu.VMEM(shape, jnp.float32),
+            pltpu.VMEM(adjacency.shape, jnp.bfloat16),
+            pltpu.VMEM(features.shape, jnp.bfloat16),
+            pltpu.SemaphoreType.DMA((2,)),
+        ],
         compiler_params=pltpu.CompilerParams(vmem_limit_bytes=32 * 2**20),
         name="collect",
     )(block_source, block_to_slot, send_counts, adjacency, features)
 
 
-def spread_kernel(source_ref, slot_ref, adj_ref, ret_ref, start_ref, out_ref, acc):
+def spread_kernel(
+    source_ref, slot_ref, adj_hbm, ret_hbm, start_hbm, hidden_in, self_in, neigh_in,
+    out_ref, hidden_out, self_out, neigh_out, acc, adj_ref, ret_ref, sems,
+):
+    loads = [
+        pltpu.make_async_copy(adj_hbm, adj_ref, sems.at[0]),
+        pltpu.make_async_copy(ret_hbm, ret_ref, sems.at[1]),
+        pltpu.make_async_copy(start_hbm, acc, sems.at[2]),
+    ]
+    results = [
+        pltpu.make_async_copy(hidden_in, hidden_out, sems.at[3]),
+        pltpu.make_async_copy(self_in, self_out, sems.at[4]),
+        pltpu.make_async_copy(neigh_in, neigh_out, sems.at[5]),
+    ]
+    for copy in loads + results:
+        copy.start()
+    for copy in loads:
+        copy.wait()
     blocks, block, _ = adj_ref.shape
     sources = out_ref.shape[0] // block
-    acc[...] = start_ref[...]
 
     def add(step, carry):
         prods = []
@@ -80,31 +107,39 @@
         return carry
 
     lax.fori_loop(0, sources, finish, 0)
-
-
-def spread(block_source, block_to_slot, adjacency, returned, self_grad):
+    for copy in results:
+        copy.wait()
+
+
+def spread(block_source, block_to_slot, adjacency, returned, self_grad, hidden, grad_self, grad_neigh):
     blocks, block, _ = adjacency.shape
     nodes, cols = self_grad.shape
     shape = (nodes // block, block, cols)
+    passed = [jax.ShapeDtypeStruct(v.shape, v.dtype) for v in (hidden, grad_self, grad_neigh)]
     return pl.pallas_call(
         spread_kernel,
-        out_shape=jax.ShapeDtypeStruct((nodes, cols), jnp.bfloat16),
-        in_specs=[pl.BlockSpec(memory_space=SMEM)] * 2 + [pl.BlockSpec(memory_space=VMEM)] * 3,
-        out_specs=pl.BlockSpec(memory_space=VMEM),
-        scratch_shapes=[pltpu.VMEM(shape, jnp.float32)],
+        out_shape=[jax.ShapeDtypeStruct((nodes, cols), jnp.bfloat16)] + passed,
+        in_specs=[pl.BlockSpec(memory_space=SMEM)] * 2 + [pl.BlockSpec(memory_space=pl.ANY)] * 6,
+        out_specs=[pl.BlockSpec(memory_space=VMEM)] + [pl.BlockSpec(memory_space=pl.ANY)] * 3,
+        scratch_shapes=[
+            pltpu.VMEM(shape, jnp.float32),
+            pltpu.VMEM(adjacency.shape, jnp.bfloat16),
+            pltpu.VMEM(returned.shape, jnp.bfloat16),
+            pltpu.SemaphoreType.DMA((6,)),
+        ],
         compiler_params=pltpu.CompilerParams(vmem_limit_bytes=32 * 2**20),
         name="spread",
-    )(block_source, block_to_slot, adjacency, returned, self_grad.reshape(shape))
+    )(block_source, block_to_slot, adjacency, returned, self_grad.reshape(shape), hidden, grad_self, grad_neigh)
 
 
 def layer_kernel(
     parts, feats,
-    out_blocks, out_ids, feat_ref, deg_ref, cot_ref, w_self, w_neigh,
+    count_ref, out_blocks, rows_ref, degree_ref, feat_hbm, cot_hbm, w_self, w_neigh,
     hidden_ref, returned_ref, self_grad_ref, grad_self_ref, grad_neigh_ref,
-    in_blocks, in_ids, sum_ref, pre_ref, feat_full, agg_full, grad_full, back_ref, back_out, back_in,
+    out_ids, deg_ref, cot_ref, in_blocks, in_ids, sum_ref, pre_ref, feat_full, agg_full, grad_full, back_ref, back_out, back_in,
     self_cols, neigh_cols, self_rows, neigh_rows, weight_acc,
     y_out, y_in, z_out, z_in, z_all, y_all,
-    a_send, a_recv, i_send, i_recv, r_send, r_recv, w_sem,
+    a_send, a_recv, i_send, i_recv, r_send, r_recv, w_sem, f_sem,
     gx_send, gs_send, gr_send, g_recv,
     ys_send, ys_recv, zs_send, zs_recv, za_send, za_recv, ya_send, ya_recv,
 ):
@@ -115,7 +150,8 @@
     x, core = f // 2, f % 2
     sibling = x * 2 + 1 - core
     z, y = g // ys, g % ys
-    nodes, cols = feat_ref.shape
+    nodes, cols = feat_hbm.shape
+    cap = out_blocks.shape[1]
     width = feats * cols
     chunk = nodes // CHUNKS
 
@@ -150,9 +186,19 @@
         pltpu.make_async_copy(w_neigh.at[:, mine], neigh_cols, w_sem.at[1]),
         pltpu.make_async_copy(w_self.at[mine, :], self_rows, w_sem.at[2]),
         pltpu.make_async_copy(w_neigh.at[mine, :], neigh_rows, w_sem.at[3]),
+        pltpu.make_async_copy(cot_hbm, cot_ref, w_sem.at[4]),
     ]
+
+    def feat_copy(c):
+        return pltpu.make_async_copy(feat_hbm.at[span(c)], feat_full.at[f, span(c)], f_sem.at[c])
+
+    loop(0, CHUNKS, lambda c: feat_copy(c).start())
     for w in weights:
         w.start()
+    for p in range(parts):
+        lane = lax.broadcasted_iota(jnp.int32, (8, cap), 1)
+        ids = jnp.broadcast_to(rows_ref[0, p:p + 1, :], (8, cap))
+        out_ids[p] = jnp.where(lane < count_ref[0, p], ids, -1)
 
     barrier = pltpu.get_barrier_semaphore()
     for d in range(1, parts):
@@ -206,6 +252,9 @@
 
     def gather_finish(n, full, c):
         arrival(n, full, c, sibling).wait_recv()
+        gather_relayed(n, full, c)
+
+    def gather_relayed(n, full, c):
         for d in range(1, chips):
             arrival(n, full, c, (x + d) % chips * 2 + 1 - core).wait_recv()
 
@@ -216,12 +265,14 @@
             relay(n, full, c, d).wait_send()
 
     def feat_start(c):
-        feat_full[f, span(c), :] = feat_ref[span(c), :]
+        feat_copy(c).wait()
         gather_start(0, feat_full, c)
 
     loop(0, CHUNKS, feat_start)
-
-    cap = out_blocks.shape[1]
+    columns = jnp.transpose(degree_ref[...].astype(jnp.float32))
+    lanes = degree_ref.shape[1]
+    for b in range(nodes // lanes):
+        deg_ref[b * lanes:(b + 1) * lanes, :] = jnp.broadcast_to(columns[:, b:b + 1], (lanes, 128))
 
     def scatter(ids, values, first):
         def tile(c):
@@ -247,7 +298,7 @@
     loop(1, parts, take_blocks)
 
     def aggregate(c):
-        agg_full[f, span(c), :] = (sum_ref[span(c), :] / deg_ref[span(c), :]).astype(jnp.bfloat16)
+        agg_full[f, span(c), :] = (sum_ref[span(c), :] / deg_ref[span(c), 0:1]).astype(jnp.bfloat16)
         gather_start(1, agg_full, c)
 
     loop(0, CHUNKS, aggregate)
@@ -278,28 +329,108 @@
 
     loop(0, CHUNKS, activate)
 
-    def weight_grads(c):
-        for j in range(feats):
-            at = slice(j * cols, (j + 1) * cols)
-            weight_acc[0:cols, at] += dot_rows(feat_ref[span(c), :], grad_full[j, span(c), :])
-            weight_acc[cols:2 * cols, at] += dot_rows(agg_full[f, span(c), :], grad_full[j, span(c), :])
+    def weight_grads(d, c):
+        q = (x + d) % chips
+        for k in range(2):
+            at = slice(k * cols, (k + 1) * cols)
+            right = grad_full[q * 2 + k, span(c), :]
+            weight_acc[d, 0:cols, at] += dot_rows(feat_full[f, span(c), :], right)
+            weight_acc[d, cols:2 * cols, at] += dot_rows(agg_full[f, span(c), :], right)
 
     def back_rows(c):
         gather_relay(2, grad_full, c)
-        gather_finish(2, grad_full, c)
+        gather_relayed(2, grad_full, c)
         total = dot_cols(grad_full[0, span(c), :], neigh_rows[:, 0:cols])
         for j in range(1, feats):
             total += dot_cols(grad_full[j, span(c), :], neigh_rows[:, j * cols:(j + 1) * cols])
-        back_ref[span(c), :] = (total / deg_ref[span(c), :]).astype(jnp.bfloat16)
+        back_ref[span(c), :] = (total / deg_ref[span(c), 0:1]).astype(jnp.bfloat16)
 
     weight_acc[...] = jnp.zeros_like(weight_acc)
 
-    def backward(c):
+    tall = 2 * cols // parts
+
+    def pieces():
+        return [(a, b, (a * zs + b) * tall) for a in range(ys) for b in range(zs)]
+
+    def y_copy(n, slot, to):
+        return remote(y_out.at[n, to], y_in.at[n, slot], ys_send.at[n, to], ys_recv.at[n, slot], z * ys + to, f)
+
+    def z_copy(n, slot, to):
+        return remote(z_out.at[n, to], z_in.at[n, slot], zs_send.at[n, to], zs_recv.at[n, slot], to * ys + y, f)
+
+    def z_gather(n, slot, to):
+        piece = z_all.at[n, slot]
+        return remote(piece, piece, za_send.at[n, to], za_recv.at[n, slot], to * ys + y, f)
+
+    def y_gather(n, slot, to):
+        piece = y_all.at[n, slot]
+        return remote(piece, piece, ya_send.at[n, to], ya_recv.at[n, slot], z * ys + to, f)
+
+    def reduce_start(n):
+        for a, b, row in pieces():
+            y_out[n, a, b] = weight_acc[n, row:row + tall, :].astype(jnp.bfloat16)
+        for d in range(1, ys):
+            y_copy(n, y, (y + d) % ys).start()
+        y_in[n, y] = y_out[n, y]
+
+    def reduce_z(n):
+        for d in range(1, ys):
+            p = (y + d) % ys
+            y_copy(n, p, p).wait_recv()
+        for b in range(zs):
+            total = y_in[n, 0, b].astype(jnp.float32)
+            for a in range(1, ys):
+                total += y_in[n, a, b].astype(jnp.float32)
+            z_out[n, b] = total.astype(jnp.bfloat16)
+        for d in range(1, zs):
+            z_copy(n, z, (z + d) % zs).start()
+        z_in[n, z] = z_out[n, z]
+
+    def finish_z(n):
+        for d in range(1, zs):
+            p = (z + d) % zs
+            z_copy(n, p, p).wait_recv()
+        total = z_in[n, 0].astype(jnp.float32)
+        for b in range(1, zs):
+            total += z_in[n, b].astype(jnp.float32)
+        z_all[n, z] = total.astype(jnp.bfloat16)
+        for d in range(1, zs):
+            z_gather(n, z, (z + d) % zs).start()
+
+    def finish_y(n):
+        for d in range(1, zs):
+            p = (z + d) % zs
+            z_gather(n, p, p).wait_recv()
+        y_all[n, y] = z_all[n]
+        for d in range(1, ys):
+            y_gather(n, y, (y + d) % ys).start()
+
+    def write_grads(n):
+        for d in range(1, ys):
+            p = (y + d) % ys
+            y_gather(n, p, p).wait_recv()
+        at = pl.ds(pl.multiple_of((x + n) % chips * 2 * cols, 2 * cols), 2 * cols)
+        for a, b, row in pieces():
+            piece = y_all[n, a, b].astype(jnp.float32)
+            if row < cols:
+                grad_self_ref[row:row + tall, at] = piece
+            else:
+                grad_neigh_ref[row - cols:row - cols + tall, at] = piece
+
+    def sibling_grads(c):
+        arrival(2, grad_full, c, sibling).wait_recv()
+        weight_grads(0, c)
+
+    stages = (reduce_z, finish_z, finish_y)
+    others = range(1, chips)
+    loop(0, CHUNKS, sibling_grads)
+    reduce_start(0)
+    for c in range(CHUNKS):
         back_rows(c)
-        weight_grads(c)
-
-    loop(0, CHUNKS - 1, backward)
-    back_rows(CHUNKS - 1)
+        for d in others:
+            weight_grads(d, c)
+        if c < len(stages):
+            stages[c](0)
 
     def pick(p):
         ids = jnp.transpose(in_ids[p])[:, 0:1]
@@ -315,29 +446,16 @@
         back_out[p] = pick(p)
         return_copy(g, p).start()
 
-    loop(1, parts, send_back)
+    for n in others:
+        reduce_start(n)
+    loop(1, parts // 2, send_back)
+    for n in others:
+        reduce_z(n)
+    loop(parts // 2, parts, send_back)
     back_in[g] = pick(g)
-    weight_grads(CHUNKS - 1)
-
-    tall, wide = 2 * cols // ys, width // zs
-    for a in range(ys):
-        for b in range(zs):
-            y_out[a, b] = weight_acc[a * tall:(a + 1) * tall, b * wide:(b + 1) * wide].astype(jnp.bfloat16)
-
-    def y_copy(slot, to):
-        return remote(y_out.at[to], y_in.at[slot], ys_send.at[to], ys_recv.at[slot], z * ys + to, f)
-
-    def z_copy(slot, to):
-        return remote(z_out.at[to], z_in.at[slot], zs_send.at[to], zs_recv.at[slot], to * ys + y, f)
-
-    def z_gather(slot, to):
-        return remote(z_all.at[slot], z_all.at[slot], za_send.at[to], za_recv.at[slot], to * ys + y, f)
-
-    def y_gather(slot, to):
-        return remote(y_all.at[slot], y_all.at[slot], ya_send.at[to], ya_recv.at[slot], z * ys + to, f)
-
-    for d in range(1, ys):
-        y_copy(y, (y + d) % ys).start()
+    returned_ref[g] = back_in[g]
+    for n in others:
+        finish_z(n)
 
     def self_part(c):
         total = dot_cols(grad_full[0, span(c), :], self_rows[:, 0:cols])
@@ -346,54 +464,18 @@
         self_grad_ref[span(c), :] = total
 
     loop(0, CHUNKS, self_part)
-    y_in[y] = y_out[y]
-    for d in range(1, ys):
-        p = (y + d) % ys
-        y_copy(p, p).wait_recv()
-    for b in range(zs):
-        total = y_in[0, b].astype(jnp.float32)
-        for a in range(1, ys):
-            total += y_in[a, b].astype(jnp.float32)
-        z_out[b] = total.astype(jnp.bfloat16)
-    for d in range(1, zs):
-        z_copy(z, (z + d) % zs).start()
-    z_in[z] = z_out[z]
-    for d in range(1, zs):
-        p = (z + d) % zs
-        z_copy(p, p).wait_recv()
-    total = z_in[0].astype(jnp.float32)
-    for b in range(1, zs):
-        total += z_in[b].astype(jnp.float32)
-    z_all[z] = total.astype(jnp.bfloat16)
-    for d in range(1, zs):
-        z_gather(z, (z + d) % zs).start()
-    for d in range(1, zs):
-        p = (z + d) % zs
-        z_gather(p, p).wait_recv()
-    y_all[y] = z_all[...]
-    for d in range(1, ys):
-        y_gather(y, (y + d) % ys).start()
+    write_grads(0)
+    for n in others:
+        finish_y(n)
 
     def returned(d):
         p = (g + parts - d) % parts
         return_copy(p, p).wait_recv()
         returned_ref[p] = back_in[p]
 
-    returned_ref[g] = back_in[g]
     loop(1, parts, returned)
-
-    for d in range(1, ys):
-        p = (y + d) % ys
-        y_gather(p, p).wait_recv()
-    for a in range(ys):
-        for b in range(zs):
-            piece = y_all[a, b].astype(jnp.float32)
-            at = slice(b * wide, (b + 1) * wide)
-            if a < ys // 2:
-                grad_self_ref[a * tall:(a + 1) * tall, at] = piece
-            else:
-                low = a - ys // 2
-                grad_neigh_ref[low * tall:(low + 1) * tall, at] = piece
+    for n in others:
+        write_grads(n)
 
     def sent(d):
         p = (g + d) % parts
@@ -404,22 +486,24 @@
     loop(1, parts, sent)
     for n, full in enumerate((feat_full, agg_full, grad_full)):
         loop(0, CHUNKS, functools.partial(gather_sent, n, full))
-    for d in range(1, ys):
-        y_copy(y, (y + d) % ys).wait_send()
-        y_gather(y, (y + d) % ys).wait_send()
-    for d in range(1, zs):
-        z_copy(z, (z + d) % zs).wait_send()
-        z_gather(z, (z + d) % zs).wait_send()
-
-
-def layer(outgoing, row_ids, features, degrees, cotangent, w_self, w_neigh):
+    for n in range(chips):
+        for d in range(1, ys):
+            y_copy(n, y, (y + d) % ys).wait_send()
+            y_gather(n, y, (y + d) % ys).wait_send()
+        for d in range(1, zs):
+            z_copy(n, z, (z + d) % zs).wait_send()
+            z_gather(n, z, (z + d) % zs).wait_send()
+
+
+def layer(send_counts, outgoing, send_rows, degrees, features, cotangent, w_self, w_neigh):
     parts, cap, cols = outgoing.shape
     nodes = features.shape[0]
     feats = lax.axis_size("feat")
     width = feats * cols
     ys = feats // 2
     zs = parts // ys
-    tall, wide = 2 * cols // ys, width // zs
+    chips = feats // 2
+    tall, wide = 2 * cols // parts, 2 * cols
     bf16, f32 = jnp.bfloat16, jnp.float32
     dma = pltpu.SemaphoreType.DMA
     hops = max(feats // 2 - 1, 1)
@@ -432,11 +516,16 @@
             jax.ShapeDtypeStruct((cols, width), f32),
             jax.ShapeDtypeStruct((cols, width), f32),
         ),
-        in_specs=[pl.BlockSpec(memory_space=VMEM)] * 5 + [pl.BlockSpec(memory_space=pl.ANY)] * 2,
+        in_specs=[pl.BlockSpec(memory_space=SMEM)]
+        + [pl.BlockSpec(memory_space=VMEM)] * 3
+        + [pl.BlockSpec(memory_space=pl.ANY)] * 4,
         out_specs=[pl.BlockSpec(memory_space=VMEM)] * 5,
         scratch_shapes=[
+            pltpu.VMEM((parts, 8, cap), jnp.int32),
+            pltpu.VMEM((nodes, 128), f32),
+            pltpu.VMEM((nodes, cols), bf16),
             pltpu.VMEM((parts, cap, cols), bf16),
-            pltpu.VMEM(row_ids.shape, jnp.int32),
+            pltpu.VMEM((parts, 8, cap), jnp.int32),
             pltpu.VMEM((nodes, cols), f32),
             pltpu.VMEM((nodes, cols), f32),
             pltpu.VMEM((feats, nodes, cols), bf16),
@@ -449,23 +538,24 @@
             pltpu.VMEM((width, cols), bf16),
             pltpu.VMEM((cols, width), bf16),
             pltpu.VMEM((cols, width), bf16),
-            pltpu.VMEM((2 * cols, width), f32),
-            pltpu.VMEM((ys, zs, tall, wide), bf16),
-            pltpu.VMEM((ys, zs, tall, wide), bf16),
-            pltpu.VMEM((zs, tall, wide), bf16),
-            pltpu.VMEM((zs, tall, wide), bf16),
-            pltpu.VMEM((zs, tall, wide), bf16),
-            pltpu.VMEM((ys, zs, tall, wide), bf16),
+            pltpu.VMEM((chips, 2 * cols, wide), f32),
+            pltpu.VMEM((chips, ys, zs, tall, wide), bf16),
+            pltpu.VMEM((chips, ys, zs, tall, wide), bf16),
+            pltpu.VMEM((chips, zs, tall, wide), bf16),
+            pltpu.VMEM((chips, zs, tall, wide), bf16),
+            pltpu.VMEM((chips, zs, tall, wide), bf16),
+            pltpu.VMEM((chips, ys, zs, tall, wide), bf16),
             dma((parts,)), dma((parts,)), dma((parts,)), dma((parts,)), dma((parts,)), dma((parts,)),
-            dma((4,)),
+            dma((5,)), dma((CHUNKS,)),
             dma((3, hops, CHUNKS)), dma((3, CHUNKS)), dma((3, hops, CHUNKS)), dma((3, feats, CHUNKS)),
-            dma((ys,)), dma((ys,)), dma((zs,)), dma((zs,)), dma((zs,)), dma((zs,)), dma((ys,)), dma((ys,)),
+            dma((chips, ys)), dma((chips, ys)), dma((chips, zs)), dma((chips, zs)),
+            dma((chips, zs)), dma((chips, zs)), dma((chips, ys)), dma((chips, ys)),
         ],
         compiler_params=pltpu.CompilerParams(
             collective_id=0, has_side_effects=True, vmem_limit_bytes=56 * 2**20
         ),
         name="layer",
-    )(outgoing, row_ids, features, degrees, cotangent, w_self, w_neigh)
+    )(send_counts, outgoing, send_rows, degrees, features, cotangent, w_self, w_neigh)
 
 
 def on_device(
@@ -486,16 +576,13 @@
     slot_cap = send_rows.shape[2]
     slot_total = part_count * slot_cap // block_size
     outgoing = collect(block_source, block_to_slot, send_counts, adjacency, features, slot_total)
-    is_live = jnp.arange(slot_cap, dtype=jnp.int32)[None, :] < send_counts[0][:, None]
-    row_ids = jnp.where(is_live, send_rows[0], -1)
-    row_ids = jnp.broadcast_to(row_ids[:, None, :], (part_count, 8, slot_cap))
-    degrees = degree.astype(jnp.float32)[:, None]
-    hidden_out, returned, self_grad, grad_self, grad_neigh = layer(
-        outgoing.reshape(part_count, slot_cap, feat_cols), row_ids, features, degrees, cotangent, w_self, w_neigh
+    hidden, returned, self_grad, grad_self, grad_neigh = layer(
+        send_counts, outgoing.reshape(part_count, slot_cap, feat_cols), send_rows,
+        degree.reshape(-1, block_size), features, cotangent, w_self, w_neigh,
     )
-    grad_features = spread(
+    grad_features, hidden_out, grad_self, grad_neigh = spread(
         block_source, block_to_slot, adjacency,
-        returned.reshape(slot_total, block_size, feat_cols), self_grad,
+        returned.reshape(slot_total, block_size, feat_cols), self_grad, hidden, grad_self, grad_neigh,
     )
     return (hidden_out, grad_features, grad_self, grad_neigh)
 

time: 174 us -> 162 us (0.931)
  the two profiles are of different devices: /device:TPU:0 before, /device:TPU:28 now
where the time goes in v3:
time: 162 us
  Pallas kernels  149 us (92%)
  local copies, waits for them, and re-layouts  11.9 us (7%)
    pallas_call x1, Pallas kernels, layer(): pl.pallas_call(functools.partial(layer_kernel, parts, feats), out_shape=(...  142 us
    unnamed x28, local copies, waits for them, and re-layouts  11.9 us
    pallas_call x1, Pallas kernels, spread(): pl.pallas_call(spread_kernel, out_shape=[jax.ShapeDtypeStruct((nodes, col...  4.13 us

profile of v3, /device:TPU:28, one launch (start us, length us, event | category | flops | bytes accessed | tf_op | source)
XLA Modules:
  0.0 162.0 jit_solution(10688061972206915383)
XLA Ops:
  0.6 0.0 copy-start
  0.6 1.2 copy-done
  1.9 0.0 copy-start.2
  1.9 1.2 copy-done.2
  3.1 0.0 copy-start.9
  3.1 0.7 copy-done.9
  3.7 0.0 copy-start.11
  3.7 0.7 copy-done.11
  4.4 0.0 copy-start.13
  4.4 0.7 copy-done.13
  5.1 3.0 %collect.1 = bf16[16,128,256]{2,1,0:T(8,128)(2,1)S(1)} custom-call(s32[32]{0:T(128)S(1)} %copy-done.9, s32[32]{0:T(128)S(1)} %copy-done.11, s32[1,8]{1,0:T(1,128)S(1)} %copy-done.13, bf16[32,128,128]{2,1,0:T(8,128)(2,1)S(1)} %copy-done, bf16[2048,256]{1,0:T(8,128)(2,1)S(1)} %copy-done.2), custom_call_target="tpu_custom_call" | custom-call | tf_op jit(solution)/shard_map/collect/pallas_call | solution.py:53
  8.1 0.0 copy-start.3
  8.1 1.0 copy-done.3
  9.0 0.0 copy-start.1
  9.0 0.0 copy-start.10
  9.0 0.0 copy-start.12
  9.1 142.3 %layer.1 = (bf16[2048,256]{1,0:T(8,128)(2,1)}, bf16[8,256,256]{2,1,0:T(8,128)(2,1)}, f32[2048,256]{1,0:T(8,128)}, f32[256,1024]{1,0:T(8,128)}, f32[256,1024]{1,0:T(8,128)}) custom-call(s32[1,8]{1,0:T(1,128)} %count_ref.3, bf16[8,256,256]{2,1,0:T(8,128)(2,1)} %bitcast.4, s32[1,8,256]{2,1,0:T(8,128)} %rows_ref.1, s32[16,128]{1,0:T(8,128)} %bitcast.7, ...), custom_call_target="tpu_custom_call" | custom-call | tf_op jit(solution)/shard_map/layer/pallas_call | solution.py:510
  151.3 0.0 copy-done.1
  151.3 0.0 copy-done.10
  151.4 0.0 copy-done.12
  151.4 0.0 copy-start.4
  151.4 1.6 copy-done.4
  153.0 0.0 copy-start.5
  153.0 1.2 copy-done.5
  154.2 0.0 copy-start.6
  154.2 1.2 copy-done.6
  155.4 0.0 copy-start.7
  155.4 1.2 copy-done.7
  156.6 0.0 copy-start.8
  156.6 1.2 copy-done.8
  157.9 4.1 %spread.1 = (bf16[2048,256]{1,0:T(8,128)(2,1)}, bf16[2048,256]{1,0:T(8,128)(2,1)}, f32[256,1024]{1,0:T(8,128)}, f32[256,1024]{1,0:T(8,128)}) custom-call(s32[32]{0:T(128)S(1)} %copy-done.10, s32[32]{0:T(128)S(1)} %copy-done.12, bf16[32,128,128]{2,1,0:T(8,128)(2,1)S(1)} %copy-done.1, bf16[16,128,256]{2,1,0:T(8,128)(2,1)S(1)} %bitcast.6, ...), custom_call_target="tpu_custom_call" | custom-call | tf_op jit(solution)/shard_map/spread/pallas_call | solution.py:119
Async XLA Ops:
  0.6 1.2 copy-start
  1.9 1.2 copy-start.2
  3.1 0.7 copy-start.9
  3.7 0.7 copy-start.11
  4.4 0.7 copy-start.13
  8.1 1.0 copy-start.3
  9.0 142.3 %copy-start.1 = (bf16[32,128,128]{2,1,0:T(8,128)(2,1)S(1)}, bf16[32,128,128]{2,1,0:T(8,128)(2,1)}, u32[]{:S(2)}) copy-start(bf16[32,128,128]{2,1,0:T(8,128)(2,1)} %adj_hbm.3) | copy-start | bytes 3145732
  9.0 142.3 %copy-start.10 = (s32[32]{0:T(128)S(1)}, s32[32]{0:T(128)}, u32[]{:S(2)}) copy-start(s32[32]{0:T(128)} %source_ref.3) | copy-start | bytes 388
  9.0 142.3 %copy-start.12 = (s32[32]{0:T(128)S(1)}, s32[32]{0:T(128)}, u32[]{:S(2)}) copy-start(s32[32]{0:T(128)} %slot_ref.3) | copy-start | bytes 388
  151.4 1.6 copy-start.4
  153.0 1.2 copy-start.5
  154.2 1.2 copy-start.6
  155.4 1.2 copy-start.7
  156.6 1.2 copy-start.8

commit v4 on v3

--- a/solution.py
+++ b/solution.py
@@ -12,6 +12,7 @@
 MESH = pl.DeviceIdType.MESH
 GROUP = 4
 CHUNKS = 4
+VMEM_BYTES = 60 * 2**20
 
 
 def collect_kernel(source_ref, slot_ref, count_ref, adj_hbm, feat_hbm, out_ref, acc, adj_ref, feat_ref, sems):
@@ -61,7 +62,7 @@
             pltpu.VMEM(features.shape, jnp.bfloat16),
             pltpu.SemaphoreType.DMA((2,)),
         ],
-        compiler_params=pltpu.CompilerParams(vmem_limit_bytes=32 * 2**20),
+        compiler_params=pltpu.CompilerParams(vmem_limit_bytes=VMEM_BYTES),
         name="collect",
     )(block_source, block_to_slot, send_counts, adjacency, features)
 
@@ -127,7 +128,7 @@
             pltpu.VMEM(returned.shape, jnp.bfloat16),
             pltpu.SemaphoreType.DMA((6,)),
         ],
-        compiler_params=pltpu.CompilerParams(vmem_limit_bytes=32 * 2**20),
+        compiler_params=pltpu.CompilerParams(vmem_limit_bytes=VMEM_BYTES),
         name="spread",
     )(block_source, block_to_slot, adjacency, returned, self_grad.reshape(shape), hidden, grad_self, grad_neigh)
 
@@ -135,11 +136,12 @@
 def layer_kernel(
     parts, feats,
     count_ref, out_blocks, rows_ref, degree_ref, feat_hbm, cot_hbm, w_self, w_neigh,
-    hidden_ref, returned_ref, self_grad_ref, grad_self_ref, grad_neigh_ref,
+    hidden_hbm, returned_hbm, self_grad_hbm, grad_self_ref, grad_neigh_ref,
     out_ids, deg_ref, cot_ref, in_blocks, in_ids, sum_ref, pre_ref, feat_full, agg_full, grad_full, back_ref, back_out, back_in,
     self_cols, neigh_cols, self_rows, neigh_rows, weight_acc,
+    self_turned, neigh_turned, left_turned, hidden_ref, self_grad_ref,
     y_out, y_in, z_out, z_in, z_all, y_all,
-    a_send, a_recv, i_send, i_recv, r_send, r_recv, w_sem, f_sem,
+    a_send, a_recv, i_send, i_recv, r_send, r_recv, w_sem, f_sem, o_sem, b_sem,
     gx_send, gs_send, gr_send, g_recv,
     ys_send, ys_recv, zs_send, zs_recv, za_send, za_recv, ya_send, ya_recv,
 ):
@@ -174,12 +176,6 @@
     def dot(a, b):
         return jnp.dot(a, b, preferred_element_type=jnp.float32)
 
-    def dot_rows(a, b):
-        return lax.dot_general(a, b, (((0,), (0,)), ((), ())), preferred_element_type=jnp.float32)
-
-    def dot_cols(a, b):
-        return lax.dot_general(a, b, (((1,), (1,)), ((), ())), preferred_element_type=jnp.float32)
-
     mine = pl.ds(pl.multiple_of(f * cols, cols), cols)
     weights = [
         pltpu.make_async_copy(w_self.at[:, mine], self_cols, w_sem.at[0]),
@@ -216,12 +212,19 @@
     def return_copy(slot, p):
         return remote(back_out.at[p], back_in.at[slot], r_send.at[p], r_recv.at[slot], p, f)
 
-    def send_blocks(d):
-        p = (g + d) % parts
+    half = parts // 2
+
+    def peer(i):
+        far = (1 - g // half) * half + (g + i) % half
+        near = g // half * half + (g + i + 1 - half) % half
+        return far * (1 - i // half) + near * (i // half)
+
+    def send_blocks(i):
+        p = peer(i)
         id_copy(g, p).start()
         block_copy(g, p).start()
 
-    loop(1, parts, send_blocks)
+    loop(0, parts - 1, send_blocks)
 
     def to_sibling(n, full, c):
         piece = full.at[f, span(c)]
@@ -289,13 +292,25 @@
     scatter(out_ids[g][0:1, :], out_blocks[g], True)
     in_ids[g] = out_ids[g]
 
-    def take_blocks(d):
-        p = (g + parts - d) % parts
+    def take_blocks(i):
+        p = peer(parts - 2 - i)
         id_copy(p, p).wait_recv()
         block_copy(p, p).wait_recv()
         scatter(in_ids[p][0:1, :], in_blocks[p], False)
 
-    loop(1, parts, take_blocks)
+    for w in weights:
+        w.wait()
+    for j in range(feats):
+        at = slice(j * cols, (j + 1) * cols)
+        self_turned[at, :] = jnp.transpose(self_rows[:, at])
+        neigh_turned[at, :] = jnp.transpose(neigh_rows[:, at])
+    weight_acc[...] = jnp.zeros_like(weight_acc)
+
+    def turn(c):
+        left_turned[0:cols, span(c)] = jnp.transpose(feat_full[f, span(c), :])
+
+    loop(0, CHUNKS, turn)
+    loop(0, parts - 1, take_blocks)
 
     def aggregate(c):
         agg_full[f, span(c), :] = (sum_ref[span(c), :] / deg_ref[span(c), 0:1]).astype(jnp.bfloat16)
@@ -303,8 +318,10 @@
 
     loop(0, CHUNKS, aggregate)
     loop(0, CHUNKS, lambda c: gather_relay(0, feat_full, c))
-    for w in weights:
-        w.wait()
+
+    def turn_aggregate(c):
+        left_turned[cols:2 * cols, span(c)] = jnp.transpose(agg_full[f, span(c), :])
+
 
     def own_term(c):
         gather_finish(0, feat_full, c)
@@ -314,6 +331,7 @@
         pre_ref[span(c), :] = total
 
     loop(0, CHUNKS, own_term)
+    loop(0, CHUNKS, turn_aggregate)
 
     def activate(c):
         gather_relay(1, agg_full, c)
@@ -328,24 +346,22 @@
         gather_start(2, grad_full, c)
 
     loop(0, CHUNKS, activate)
+    hidden_copy = pltpu.make_async_copy(hidden_ref, hidden_hbm, o_sem.at[0])
+    hidden_copy.start()
 
     def weight_grads(d, c):
         q = (x + d) % chips
         for k in range(2):
             at = slice(k * cols, (k + 1) * cols)
-            right = grad_full[q * 2 + k, span(c), :]
-            weight_acc[d, 0:cols, at] += dot_rows(feat_full[f, span(c), :], right)
-            weight_acc[d, cols:2 * cols, at] += dot_rows(agg_full[f, span(c), :], right)
+            weight_acc[d, :, at] += dot(left_turned[:, span(c)], grad_full[q * 2 + k, span(c), :])
 
     def back_rows(c):
         gather_relay(2, grad_full, c)
         gather_relayed(2, grad_full, c)
-        total = dot_cols(grad_full[0, span(c), :], neigh_rows[:, 0:cols])
+        total = dot(grad_full[0, span(c), :], neigh_turned[0:cols, :])
         for j in range(1, feats):
-            total += dot_cols(grad_full[j, span(c), :], neigh_rows[:, j * cols:(j + 1) * cols])
+            total += dot(grad_full[j, span(c), :], neigh_turned[j * cols:(j + 1) * cols, :])
         back_ref[span(c), :] = (total / deg_ref[span(c), 0:1]).astype(jnp.bfloat16)
-
-    weight_acc[...] = jnp.zeros_like(weight_acc)
 
     tall = 2 * cols // parts
 
@@ -441,41 +457,51 @@
             total += dot(match, back_ref[c * chunk:(c + 1) * chunk, :])
         return total.astype(jnp.bfloat16)
 
-    def send_back(d):
-        p = (g + d) % parts
+    def send_back(i):
+        p = peer(i)
         back_out[p] = pick(p)
         return_copy(g, p).start()
 
+
+    def keep(p):
+        return pltpu.make_async_copy(back_in.at[p], returned_hbm.at[p], b_sem.at[p])
+
     for n in others:
         reduce_start(n)
-    loop(1, parts // 2, send_back)
+    loop(0, half, send_back)
     for n in others:
         reduce_z(n)
-    loop(parts // 2, parts, send_back)
+    loop(half, parts - 1, send_back)
     back_in[g] = pick(g)
-    returned_ref[g] = back_in[g]
+    keep(g).start()
     for n in others:
         finish_z(n)
 
     def self_part(c):
-        total = dot_cols(grad_full[0, span(c), :], self_rows[:, 0:cols])
+        total = dot(grad_full[0, span(c), :], self_turned[0:cols, :])
         for j in range(1, feats):
-            total += dot_cols(grad_full[j, span(c), :], self_rows[:, j * cols:(j + 1) * cols])
+            total += dot(grad_full[j, span(c), :], self_turned[j * cols:(j + 1) * cols, :])
         self_grad_ref[span(c), :] = total
 
     loop(0, CHUNKS, self_part)
+    self_copy = pltpu.make_async_copy(self_grad_ref, self_grad_hbm, o_sem.at[1])
+    self_copy.start()
     write_grads(0)
     for n in others:
         finish_y(n)
 
-    def returned(d):
-        p = (g + parts - d) % parts
+    def returned(i):
+        p = peer(parts - 2 - i)
         return_copy(p, p).wait_recv()
-        returned_ref[p] = back_in[p]
-
-    loop(1, parts, returned)
+        keep(p).start()
+
+    loop(0, parts - 1, returned)
     for n in others:
         write_grads(n)
+
+    hidden_copy.wait()
+    self_copy.wait()
+    loop(0, parts, lambda p: keep(p).wait())
 
     def sent(d):
         p = (g + d) % parts
@@ -519,7 +545,7 @@
         in_specs=[pl.BlockSpec(memory_space=SMEM)]
         + [pl.BlockSpec(memory_space=VMEM)] * 3
         + [pl.BlockSpec(memory_space=pl.ANY)] * 4,
-        out_specs=[pl.BlockSpec(memory_space=VMEM)] * 5,
+        out_specs=[pl.BlockSpec(memory_space=pl.ANY)] * 3 + [pl.BlockSpec(memory_space=VMEM)] * 2,
         scratch_shapes=[
             pltpu.VMEM((parts, 8, cap), jnp.int32),
             pltpu.VMEM((nodes, 128), f32),
@@ -539,6 +565,11 @@
             pltpu.VMEM((cols, width), bf16),
             pltpu.VMEM((cols, width), bf16),
             pltpu.VMEM((chips, 2 * cols, wide), f32),
+            pltpu.VMEM((width, cols), bf16),
+            pltpu.VMEM((width, cols), bf16),
+            pltpu.VMEM((2 * cols, nodes), bf16),
+            pltpu.VMEM((nodes, cols), bf16),
+            pltpu.VMEM((nodes, cols), f32),
             pltpu.VMEM((chips, ys, zs, tall, wide), bf16),
             pltpu.VMEM((chips, ys, zs, tall, wide), bf16),
             pltpu.VMEM((chips, zs, tall, wide), bf16),
@@ -546,13 +577,13 @@
             pltpu.VMEM((chips, zs, tall, wide), bf16),
             pltpu.VMEM((chips, ys, zs, tall, wide), bf16),
             dma((parts,)), dma((parts,)), dma((parts,)), dma((parts,)), dma((parts,)), dma((parts,)),
-            dma((5,)), dma((CHUNKS,)),
+            dma((5,)), dma((CHUNKS,)), dma((2,)), dma((parts,)),
             dma((3, hops, CHUNKS)), dma((3, CHUNKS)), dma((3, hops, CHUNKS)), dma((3, feats, CHUNKS)),
             dma((chips, ys)), dma((chips, ys)), dma((chips, zs)), dma((chips, zs)),
             dma((chips, zs)), dma((chips, zs)), dma((chips, ys)), dma((chips, ys)),
         ],
         compiler_params=pltpu.CompilerParams(
-            collective_id=0, has_side_effects=True, vmem_limit_bytes=56 * 2**20
+            collective_id=0, has_side_effects=True, vmem_limit_bytes=VMEM_BYTES
         ),
         name="layer",
     )(send_counts, outgoing, send_rows, degrees, features, cotangent, w_self, w_neigh)

time: 162 us -> 238 us (1.47)
  the two profiles are of different devices: /device:TPU:28 before, /device:TPU:0 now
where the time goes in v4:
time: 238 us
  Pallas kernels  238 us (100%)
    pallas_call x1, Pallas kernels, layer(): pl.pallas_call(functools.partial(layer_kernel, parts, feats), out_shape=(...  134 us
    pallas_call x1, Pallas kernels, spread(): pl.pallas_call(spread_kernel, out_shape=[jax.ShapeDtypeStruct((nodes, col...  98.1 us
    pallas_call x1, Pallas kernels, collect(): pl.pallas_call(collect_kernel, out_shape=jax.ShapeDtypeStruct(shape, jnp....  5.37 us

profile of v4, /device:TPU:0, one launch (start us, length us, event | category | flops | bytes accessed | tf_op | source)
XLA Modules:
  0.0 238.3 jit_solution(11996980866229937965)
XLA Ops:
  0.6 5.4 %collect.1 = bf16[16,128,256]{2,1,0:T(8,128)(2,1)} custom-call(s32[32]{0:T(128)} %source_ref.3, s32[32]{0:T(128)} %slot_ref.3, s32[1,8]{1,0:T(1,128)} %count_ref.3, bf16[32,128,128]{2,1,0:T(8,128)(2,1)} %adj_hbm.3, bf16[2048,256]{1,0:T(8,128)(2,1)} %feat_hbm.3), custom_call_target="tpu_custom_call" | custom-call | tf_op jit(solution)/shard_map/collect/pallas_call | solution.py:54
  6.0 134.2 %layer.1 = (bf16[2048,256]{1,0:T(8,128)(2,1)}, bf16[8,256,256]{2,1,0:T(8,128)(2,1)}, f32[2048,256]{1,0:T(8,128)}, f32[256,1024]{1,0:T(8,128)}, f32[256,1024]{1,0:T(8,128)}) custom-call(s32[1,8]{1,0:T(1,128)} %count_ref.3, bf16[8,256,256]{2,1,0:T(8,128)(2,1)} %bitcast.4, s32[1,8,256]{2,1,0:T(8,128)} %rows_ref.1, s32[16,128]{1,0:T(8,128)} %bitcast.7, ...), custom_call_target="tpu_custom_call" | custom-call | tf_op jit(solution)/shard_map/layer/pallas_call | solution.py:536
  140.2 98.1 %spread.1 = (bf16[2048,256]{1,0:T(8,128)(2,1)}, bf16[2048,256]{1,0:T(8,128)(2,1)}, f32[256,1024]{1,0:T(8,128)}, f32[256,1024]{1,0:T(8,128)}) custom-call(s32[32]{0:T(128)} %source_ref.3, s32[32]{0:T(128)} %slot_ref.3, bf16[32,128,128]{2,1,0:T(8,128)(2,1)} %adj_hbm.3, bf16[16,128,256]{2,1,0:T(8,128)(2,1)} %bitcast.6, f32[16,128,256]{2,1,0:T(8,128)} %bitcast.5, ...), custom_call_target="tpu_custom_call" | custom-call | tf_op jit(solution)/shard_map/spread/pallas_call | solution.py:120

commit v5 on v4

--- a/solution.py
+++ b/solution.py
@@ -69,22 +69,30 @@
 
 def spread_kernel(
     source_ref, slot_ref, adj_hbm, ret_hbm, start_hbm, hidden_in, self_in, neigh_in,
-    out_ref, hidden_out, self_out, neigh_out, acc, adj_ref, ret_ref, sems,
+    out_ref, hidden_out, self_out, neigh_out, acc, adj_ref, ret_ref, hidden_ref, self_ref, neigh_ref, sems,
 ):
     loads = [
         pltpu.make_async_copy(adj_hbm, adj_ref, sems.at[0]),
         pltpu.make_async_copy(ret_hbm, ret_ref, sems.at[1]),
         pltpu.make_async_copy(start_hbm, acc, sems.at[2]),
     ]
+    passed = [
+        pltpu.make_async_copy(hidden_in, hidden_ref, sems.at[3]),
+        pltpu.make_async_copy(self_in, self_ref, sems.at[4]),
+        pltpu.make_async_copy(neigh_in, neigh_ref, sems.at[5]),
+    ]
     results = [
-        pltpu.make_async_copy(hidden_in, hidden_out, sems.at[3]),
-        pltpu.make_async_copy(self_in, self_out, sems.at[4]),
-        pltpu.make_async_copy(neigh_in, neigh_out, sems.at[5]),
+        pltpu.make_async_copy(hidden_ref, hidden_out, sems.at[6]),
+        pltpu.make_async_copy(self_ref, self_out, sems.at[7]),
+        pltpu.make_async_copy(neigh_ref, neigh_out, sems.at[8]),
     ]
-    for copy in loads + results:
+    for copy in loads + passed:
         copy.start()
     for copy in loads:
         copy.wait()
+    for first, second in zip(passed, results):
+        first.wait()
+        second.start()
     blocks, block, _ = adj_ref.shape
     sources = out_ref.shape[0] // block
 
@@ -126,7 +134,10 @@
             pltpu.VMEM(shape, jnp.float32),
             pltpu.VMEM(adjacency.shape, jnp.bfloat16),
             pltpu.VMEM(returned.shape, jnp.bfloat16),
-            pltpu.SemaphoreType.DMA((6,)),
+            pltpu.VMEM(hidden.shape, hidden.dtype),
+            pltpu.VMEM(grad_self.shape, grad_self.dtype),
+            pltpu.VMEM(grad_neigh.shape, grad_neigh.dtype),
+            pltpu.SemaphoreType.DMA((9,)),
         ],
         compiler_params=pltpu.CompilerParams(vmem_limit_bytes=VMEM_BYTES),
         name="spread",
@@ -333,6 +344,22 @@
     loop(0, CHUNKS, own_term)
     loop(0, CHUNKS, turn_aggregate)
 
+    def weight_grads(d, c):
+        q = (x + d) % chips
+        for k in range(2):
+            at = slice(k * cols, (k + 1) * cols)
+            weight_acc[d, :, at] += dot(left_turned[:, span(c)], grad_full[q * 2 + k, span(c), :])
+
+    def sibling_grads(c):
+        arrival(2, grad_full, c, sibling).wait_recv()
+        weight_grads(0, c)
+
+    def self_part(c):
+        total = dot(grad_full[0, span(c), :], self_turned[0:cols, :])
+        for j in range(1, feats):
+            total += dot(grad_full[j, span(c), :], self_turned[j * cols:(j + 1) * cols, :])
+        self_grad_ref[span(c), :] = total
+
     def activate(c):
         gather_relay(1, agg_full, c)
         gather_finish(1, agg_full, c)
@@ -345,15 +372,16 @@
         grad_full[f, span(c), :] = (cot_ref[span(c), :].astype(jnp.float32) * slope).astype(jnp.bfloat16)
         gather_start(2, grad_full, c)
 
-    loop(0, CHUNKS, activate)
+    activate(0)
+
+    def activate_next(c):
+        sibling_grads(c - 1)
+        activate(c)
+
+    loop(1, CHUNKS, activate_next)
+    sibling_grads(CHUNKS - 1)
     hidden_copy = pltpu.make_async_copy(hidden_ref, hidden_hbm, o_sem.at[0])
     hidden_copy.start()
-
-    def weight_grads(d, c):
-        q = (x + d) % chips
-        for k in range(2):
-            at = slice(k * cols, (k + 1) * cols)
-            weight_acc[d, :, at] += dot(left_turned[:, span(c)], grad_full[q * 2 + k, span(c), :])
 
     def back_rows(c):
         gather_relay(2, grad_full, c)
@@ -433,13 +461,8 @@
             else:
                 grad_neigh_ref[row - cols:row - cols + tall, at] = piece
 
-    def sibling_grads(c):
-        arrival(2, grad_full, c, sibling).wait_recv()
-        weight_grads(0, c)
-
-    stages = (reduce_z, finish_z, finish_y)
+    stages = (reduce_z, finish_z)
     others = range(1, chips)
-    loop(0, CHUNKS, sibling_grads)
     reduce_start(0)
     for c in range(CHUNKS):
         back_rows(c)
@@ -447,6 +470,8 @@
             weight_grads(d, c)
         if c < len(stages):
             stages[c](0)
+        if c < CHUNKS - 1:
+            self_part(c)
 
     def pick(p):
         ids = jnp.transpose(in_ids[p])[:, 0:1]
@@ -469,6 +494,7 @@
     for n in others:
         reduce_start(n)
     loop(0, half, send_back)
+    finish_y(0)
     for n in others:
         reduce_z(n)
     loop(half, parts - 1, send_back)
@@ -477,13 +503,7 @@
     for n in others:
         finish_z(n)
 
-    def self_part(c):
-        total = dot(grad_full[0, span(c), :], self_turned[0:cols, :])
-        for j in range(1, feats):
-            total += dot(grad_full[j, span(c), :], self_turned[j * cols:(j + 1) * cols, :])
-        self_grad_ref[span(c), :] = total
-
-    loop(0, CHUNKS, self_part)
+    self_part(CHUNKS - 1)
     self_copy = pltpu.make_async_copy(self_grad_ref, self_grad_hbm, o_sem.at[1])
     self_copy.start()
     write_grads(0)

time: 238 us -> 143 us (0.60)
  Pallas kernels: 238 us -> 142 us
    pallas_call x1, Pallas kernels: 98.1 us -> 7.11 us  [spread(): pl.pallas_call(spread_kernel, out_shape=[jax.ShapeDtypeStruct((nodes, col...]
    pallas_call x1, Pallas kernels: 134 us -> 130 us  [layer(): pl.pallas_call(functools.partial(layer_kernel, parts, feats), out_shape=(...]
where the time goes in v5:
time: 143 us
  Pallas kernels  142 us (99%)
    pallas_call x1, Pallas kernels, layer(): pl.pallas_call(functools.partial(layer_kernel, parts, feats), out_shape=(...  130 us
    pallas_call x1, Pallas kernels, spread(): pl.pallas_call(spread_kernel, out_shape=[jax.ShapeDtypeStruct((nodes, col...  7.11 us
    pallas_call x1, Pallas kernels, collect(): pl.pallas_call(collect_kernel, out_shape=jax.ShapeDtypeStruct(shape, jnp....  5.37 us

profile of v5, /device:TPU:0, one launch (start us, length us, event | category | flops | bytes accessed | tf_op | source)
XLA Modules:
  0.0 142.7 jit_solution(7037341042019462594)
XLA Ops:
  0.6 5.4 %collect.1 = bf16[16,128,256]{2,1,0:T(8,128)(2,1)} custom-call(s32[32]{0:T(128)} %source_ref.3, s32[32]{0:T(128)} %slot_ref.3, s32[1,8]{1,0:T(1,128)} %count_ref.3, bf16[32,128,128]{2,1,0:T(8,128)(2,1)} %adj_hbm.3, bf16[2048,256]{1,0:T(8,128)(2,1)} %feat_hbm.3), custom_call_target="tpu_custom_call" | custom-call | tf_op jit(solution)/shard_map/collect/pallas_call | solution.py:54
  6.0 129.5 %layer.1 = (bf16[2048,256]{1,0:T(8,128)(2,1)}, bf16[8,256,256]{2,1,0:T(8,128)(2,1)}, f32[2048,256]{1,0:T(8,128)}, f32[256,1024]{1,0:T(8,128)}, f32[256,1024]{1,0:T(8,128)}) custom-call(s32[1,8]{1,0:T(1,128)} %count_ref.3, bf16[8,256,256]{2,1,0:T(8,128)(2,1)} %bitcast.4, s32[1,8,256]{2,1,0:T(8,128)} %rows_ref.1, s32[16,128]{1,0:T(8,128)} %bitcast.7, ...), custom_call_target="tpu_custom_call" | custom-call | tf_op jit(solution)/shard_map/layer/pallas_call | solution.py:556
  135.5 7.1 %spread.1 = (bf16[2048,256]{1,0:T(8,128)(2,1)}, bf16[2048,256]{1,0:T(8,128)(2,1)}, f32[256,1024]{1,0:T(8,128)}, f32[256,1024]{1,0:T(8,128)}) custom-call(s32[32]{0:T(128)} %source_ref.3, s32[32]{0:T(128)} %slot_ref.3, bf16[32,128,128]{2,1,0:T(8,128)(2,1)} %adj_hbm.3, bf16[16,128,256]{2,1,0:T(8,128)(2,1)} %bitcast.6, f32[16,128,256]{2,1,0:T(8,128)} %bitcast.5, ...), custom_call_target="tpu_custom_call" | custom-call | tf_op jit(solution)/shard_map/spread/pallas_call | solution.py:128

commit v6 on v5

--- a/solution.py
+++ b/solution.py
@@ -86,10 +86,12 @@
         pltpu.make_async_copy(self_ref, self_out, sems.at[7]),
         pltpu.make_async_copy(neigh_ref, neigh_out, sems.at[8]),
     ]
-    for copy in loads + passed:
+    for copy in loads:
         copy.start()
     for copy in loads:
         copy.wait()
+    for copy in passed:
+        copy.start()
     for first, second in zip(passed, results):
         first.wait()
         second.start()
@@ -493,7 +495,7 @@
 
     for n in others:
         reduce_start(n)
-    loop(0, half, send_back)
+    loop(0, half - 1, send_back)
     finish_y(0)
     for n in others:
         reduce_z(n)
@@ -502,6 +504,7 @@
     keep(g).start()
     for n in others:
         finish_z(n)
+    send_back(half - 1)
 
     self_part(CHUNKS - 1)
     self_copy = pltpu.make_async_copy(self_grad_ref, self_grad_hbm, o_sem.at[1])

time: 143 us -> 143 us (level); the launches traced: 143 us -> 141 us
  Pallas kernels: 142 us -> 140 us
    pallas_call x1, Pallas kernels: 130 us -> 127 us  [layer(): pl.pallas_call(functools.partial(layer_kernel, parts, feats), out_shape=(...]
where the time goes in v6:
time: 143 us; the launch traced here: 141 us
  Pallas kernels  140 us (98%)
    pallas_call x1, Pallas kernels, layer(): pl.pallas_call(functools.partial(layer_kernel, parts, feats), out_shape=(...  127 us
    pallas_call x1, Pallas kernels, spread(): pl.pallas_call(spread_kernel, out_shape=[jax.ShapeDtypeStruct((nodes, col...  8.1 us
    pallas_call x1, Pallas kernels, collect(): pl.pallas_call(collect_kernel, out_shape=jax.ShapeDtypeStruct(shape, jnp....  5.37 us

profile of v6, /device:TPU:0, one launch (start us, length us, event | category | flops | bytes accessed | tf_op | source)
XLA Modules:
  0.0 141.0 jit_solution(15611898564519003670)
XLA Ops:
  0.6 5.4 %collect.1 = bf16[16,128,256]{2,1,0:T(8,128)(2,1)} custom-call(s32[32]{0:T(128)} %source_ref.3, s32[32]{0:T(128)} %slot_ref.3, s32[1,8]{1,0:T(1,128)} %count_ref.3, bf16[32,128,128]{2,1,0:T(8,128)(2,1)} %adj_hbm.3, bf16[2048,256]{1,0:T(8,128)(2,1)} %feat_hbm.3), custom_call_target="tpu_custom_call" | custom-call | tf_op jit(solution)/shard_map/collect/pallas_call | solution.py:54
  6.0 126.8 %layer.1 = (bf16[2048,256]{1,0:T(8,128)(2,1)}, bf16[8,256,256]{2,1,0:T(8,128)(2,1)}, f32[2048,256]{1,0:T(8,128)}, f32[256,1024]{1,0:T(8,128)}, f32[256,1024]{1,0:T(8,128)}) custom-call(s32[1,8]{1,0:T(1,128)} %count_ref.3, bf16[8,256,256]{2,1,0:T(8,128)(2,1)} %bitcast.4, s32[1,8,256]{2,1,0:T(8,128)} %rows_ref.1, s32[16,128]{1,0:T(8,128)} %bitcast.7, ...), custom_call_target="tpu_custom_call" | custom-call | tf_op jit(solution)/shard_map/layer/pallas_call | solution.py:559
  132.9 8.1 %spread.1 = (bf16[2048,256]{1,0:T(8,128)(2,1)}, bf16[2048,256]{1,0:T(8,128)(2,1)}, f32[256,1024]{1,0:T(8,128)}, f32[256,1024]{1,0:T(8,128)}) custom-call(s32[32]{0:T(128)} %source_ref.3, s32[32]{0:T(128)} %slot_ref.3, bf16[32,128,128]{2,1,0:T(8,128)(2,1)} %adj_hbm.3, bf16[16,128,256]{2,1,0:T(8,128)(2,1)} %bitcast.6, f32[16,128,256]{2,1,0:T(8,128)} %bitcast.5, ...), custom_call_target="tpu_custom_call" | custom-call | tf_op jit(solution)/shard_map/spread/pallas_call | solution.py:130
